TPU v7x, 512 devices: a whole 4x8x8 slice. The times are simulated.
512 devices in a mesh: island: 8 (over y_lo, x), fsdp: 64 (over z, y_hi, core).
Axes of the slice: x: 4, y: 8 (y_hi: 4, y_lo: 2; y = y_hi * 2 + y_lo), z: 8, core: 2. Of those that a mesh axis runs over, the one named last changes fastest.
Arguments:
- tokens: bfloat16 [262144, 4096], P(('island', 'fsdp')), may hold values from -24 to 24
- target: bfloat16 [262144, 128], P(('island', 'fsdp')), may hold values from -6 to 6
- weight: float32 [8, 4096, 128], P('island', 'fsdp'), may hold values from -6 to 6
- gain: float32 [8, 4096], P('island', 'fsdp'), may hold values from 0.25 to 1.75
- first_weight: float32 [8, 4096, 128], P('island', 'fsdp'), may hold values from -6 to 6
- second_weight: float32 [8, 4096, 128], P('island', 'fsdp'), may hold values from 0.1 to 2
- first_gain: float32 [8, 4096], P('island', 'fsdp'), may hold values from -18 to 18
- second_gain: float32 [8, 4096], P('island', 'fsdp'), may hold values from 104857 to 2097152
- anchor: float32 [4096, 128], P('fsdp'), may hold values from -6 to 6
- snapshot: float32 [8, 4096, 128], P('island', 'fsdp'), may hold values from -6 to 6
- momentum: float32 [4096, 128], P('fsdp'), may hold values from -6 to 6
Outputs:
- values: bfloat16 [262144, 128], P(('island', 'fsdp'))
- weight_new: float32 [8, 4096, 128], P('island', 'fsdp')
- gain_new: float32 [8, 4096], P('island', 'fsdp')
- first_weight_new: float32 [8, 4096, 128], P('island', 'fsdp')
- second_weight_new: float32 [8, 4096, 128], P('island', 'fsdp')
- first_gain_new: float32 [8, 4096], P('island', 'fsdp')
- second_gain_new: float32 [8, 4096], P('island', 'fsdp')
- anchor_new: float32 [4096, 128], P('fsdp')
- momentum_new: float32 [4096, 128], P('fsdp')
All inputs are finite; a program needn't handle non-finite values.
Results may differ from a plain program's by a relative error of at most 0.02.
Values may be sent and summed in bfloat16 or wider, within the bound.
A program may use at most 64 MiB of HBM per device.

v0:
```python
import jax
import jax.numpy as jnp
from jax import lax
from jax.sharding import PartitionSpec as P

D = 4096


def adamw(param, grad, first, second):
    first_next = 0.9 * first + 0.1 * grad
    second_next = 0.95 * second + 0.05 * grad * grad
    inner = param - 0.01 * (first_next / (jnp.sqrt(second_next) + 1e-08) + 0.1 * param)
    return (inner, first_next, second_next)


def outer_math(delta_sum, momentum_part, anchor_part, islands):
    mean_delta = delta_sum / islands
    momentum_next = 0.9 * momentum_part + mean_delta
    anchor_next = anchor_part - 0.7 * (mean_delta + 0.9 * momentum_next)
    return (momentum_next, anchor_next)


def per_device(
    tokens,
    target,
    weight,
    gain,
    first_weight,
    second_weight,
    first_gain,
    second_gain,
    anchor,
    snapshot,
    momentum,
):
    scale = 1.0 / float(D) ** 0.5
    local_weight = weight[0]
    local_gain = gain[0]
    wide = tokens.astype(jnp.float32)
    rstd = lax.rsqrt(jnp.mean(wide * wide, axis=1, keepdims=True) + 1e-05)
    normed = (wide * rstd).astype(jnp.bfloat16)
    effective = (local_gain[:, None] * local_weight * scale).astype(jnp.bfloat16)
    columns = normed
    projected = jnp.dot(
        columns,
        lax.all_gather(effective, "fsdp", axis=0, tiled=True),
        preferred_element_type=jnp.float32,
    )
    values = projected.astype(jnp.bfloat16)
    error = (projected - target.astype(jnp.float32)).astype(jnp.bfloat16)
    contract = (((0,), (0,)), ((), ()))
    columns = normed
    summed = lax.psum_scatter(
        lax.dot_general(columns, error, contract, preferred_element_type=jnp.float32),
        "fsdp",
        scatter_dimension=0,
        tiled=True,
    )
    grad_weight = local_gain[:, None] * summed * scale
    grad_gain = jnp.sum(local_weight * summed, axis=1) * scale
    inner_weight, first_w, second_w = adamw(
        local_weight, grad_weight, first_weight[0], second_weight[0]
    )
    inner_gain, first_g, second_g = adamw(local_gain, grad_gain, first_gain[0], second_gain[0])
    delta = (anchor - snapshot[0]).astype(jnp.bfloat16)
    islands = lax.axis_size("island")
    delta_sum = lax.psum(delta, "island").astype(jnp.float32)
    momentum_new, anchor_new = outer_math(delta_sum, momentum, anchor, islands)
    weight_new = 0.5 * inner_weight + 0.5 * anchor_new
    return (
        values,
        weight_new[None],
        inner_gain[None],
        first_w[None],
        second_w[None],
        first_g[None],
        second_g[None],
        anchor_new,
        momentum_new,
    )


def solution(mesh):
    placed = (
        P(("island", "fsdp"), None),
        P(("island", "fsdp"), None),
        P("island", "fsdp", None),
        P("island", "fsdp"),
        P("island", "fsdp", None),
        P("island", "fsdp", None),
        P("island", "fsdp"),
        P("island", "fsdp"),
        P("fsdp", None),
        P("island", "fsdp", None),
        P("fsdp", None),
    )
    return jax.shard_map(
        per_device,
        mesh=mesh,
        in_specs=placed,
        out_specs=(
            P(("island", "fsdp"), None),
            P("island", "fsdp", None),
            P("island", "fsdp"),
            P("island", "fsdp", None),
            P("island", "fsdp", None),
            P("island", "fsdp"),
            P("island", "fsdp"),
            P("fsdp", None),
            P("fsdp", None),
        ),
        check_vma=False,
    )
```

profile of v0, /device:TPU:1, one launch (start us, length us, event | category | flops | bytes accessed | tf_op | source)
XLA Modules:
  0.0 260.7 jit_solution(3125921043372186238)
XLA Ops:
  7.2 0.0 all-gather.2.cloned.1.call-start
  7.2 1.4 fusion.8
  8.7 0.0 all-gather.2.cloned.1.call-update
  8.7 0.0 reduce-scatter.2.cloned.1.call-start
  8.7 3.1 %fusion = f32[512]{0:T(512)S(1)} fusion(bf16[512,4096]{1,0:T(8,128)(2,1)} %param.11), kind=kLoop, calls=%fused_computation.2 | loop fusion | flops 6290944 | bytes 4196352 | tf_op jit(solution)/shard_map/reduce_sum | solution.py:40
  11.8 0.0 copy-start.10
  11.8 89.1 %all-gather.2.cloned.1.call-done = bf16[4096,128]{1,0:T(8,128)(2,1)} async-done(((bf16[64,128]{1,0:T(8,128)(2,1)}), bf16[4096,128]{1,0:T(8,128)(2,1)}) %all-gather.2.cloned.1.call-update) | async-done | bytes 1048592 | tf_op jit(solution)/shard_map/all_gather | solution.py:46
  100.9 0.0 copy-start
  101.0 4.6 %fusion.17 = (bf16[512,128]{1,0:T(8,128)(2,1)}, f32[512,128]{1,0:T(8,128)S(1)}) fusion(bf16[4096,128]{1,0:T(8,128)(2,1)} %all-gather.2.cloned.1.call-done, bf16[512,4096]{1,0:T(8,128)(2,1)} %param.11, f32[512]{0:T(512)S(1)} %add_rsqrt_fusion), kind=kOutput, calls=%fused_computation.32 | convolution fusion | flops 543227904 | bytes 5638144 | tf_op jit(solution)/shard_map/dot_general | solution.py:44
  105.5 0.0 copy-done.10
  105.5 0.0 copy-done
  105.5 0.0 copy-start.2
  105.5 0.0 copy-start.6
  105.6 0.0 copy-start.1
  105.6 0.0 copy-start.3
  105.6 0.0 copy-start.4
  105.6 0.0 copy-start.5
  105.6 0.0 copy-start.7
  105.6 0.0 copy-start.8
  105.6 0.0 copy-start.9
  105.6 3.4 %fusion.2 = f32[4096,128]{1,0:T(8,128)} fusion(bf16[512,4096]{1,0:T(8,128)(2,1)S(1)} %copy-done, f32[512]{0:T(512)S(1)} %add_rsqrt_fusion, f32[512,128]{1,0:T(8,128)S(1)} %get-tuple-element.19, bf16[512,128]{1,0:T(8,128)(2,1)S(1)} %copy-done.10), kind=kOutput, calls=%fused_computation.4 | convolution fusion | flops 543358976 | bytes 6686720 | tf_op jit(solution)/shard_map/dot_general | solution.py:54
  109.0 0.0 reduce-scatter.2.cloned.1.call-update
  109.0 0.0 copy-done.2
  109.0 0.0 copy-done.6
  109.1 26.3 %psum.7 = bf16[64,128]{1,0:T(8,128)(2,1)S(1)} all-reduce(bf16[64,128]{1,0:T(8,128)(2,1)S(1)} %fusion.6), channel_id=1, replica_groups=mesh['island'=8,'fsdp'=64] {'island'}, use_global_device_ids=true, to_apply=%region_2.0 | all-reduce | flops 8192 | bytes 32768 | tf_op jit(solution)/shard_map/psum | solution.py:67
  135.3 116.3 %reduce-scatter.2.cloned.1.call-done = f32[64,128]{1,0:T(8,128)} async-done(((f32[4096,128]{1,0:T(8,128)}), f32[64,128]{1,0:T(8,128)}) %reduce-scatter.2.cloned.1.call-update) | async-done | bytes 32784 | tf_op jit(solution)/shard_map/reduce_scatter | solution.py:53
  251.6 0.0 copy-done.1
  251.6 0.0 copy-done.3
  251.7 0.0 copy-done.4
  251.7 0.0 copy-done.5
  251.7 0.0 copy-done.7
  251.7 1.6 fusion.13
  253.3 0.0 copy-done.8
  253.3 0.0 copy-done.9
  253.3 0.5 multiply_subtract_fusion.1
  (2 shorter events, 0.0 us)
Async XLA Ops:
  7.2 93.8 %all-gather.2.cloned.1.call-start = ((), (), s32[]{:S(2)}) async-start(), calls=%async_computation.1 | async-start | bytes 1064960 | tf_op jit(solution)/shard_map/all_gather | solution.py:46
  8.7 243.0 %reduce-scatter.2.cloned.1.call-start = ((), (), s32[]{:S(2)}) async-start(), calls=%async_computation.2 | async-start | bytes 2129920 | tf_op jit(solution)/shard_map/reduce_scatter | solution.py:53
  11.8 93.7 %copy-start.10 = (bf16[512,128]{1,0:T(8,128)(2,1)S(1)}, bf16[512,128]{1,0:T(8,128)(2,1)}, u32[]{:S(2)}) copy-start(bf16[512,128]{1,0:T(8,128)(2,1)} %param.12) | copy-start | bytes 393220
  100.9 4.6 %copy-start = (bf16[512,4096]{1,0:T(8,128)(2,1)S(1)}, bf16[512,4096]{1,0:T(8,128)(2,1)}, u32[]{:S(2)}) copy-start(bf16[512,4096]{1,0:T(8,128)(2,1)} %param.11) | copy-start | bytes 12582916
  105.5 3.5 %copy-start.2 = (f32[64,128]{1,0:T(8,128)S(1)}, f32[64,128]{1,0:T(8,128)}, u32[]{:S(2)}) copy-start(f32[64,128]{1,0:T(8,128)} %param.19) | copy-start | bytes 98308
  105.5 3.5 %copy-start.6 = (f32[1,64,128]{2,1,0:T(8,128)S(1)}, f32[1,64,128]{2,1,0:T(8,128)}, u32[]{:S(2)}) copy-start(f32[1,64,128]{2,1,0:T(8,128)} %param.20) | copy-start | bytes 98308
  105.6 146.1 %copy-start.1 = (f32[1,64,128]{2,1,0:T(8,128)S(1)}, f32[1,64,128]{2,1,0:T(8,128)}, u32[]{:S(2)}) copy-start(f32[1,64,128]{2,1,0:T(8,128)} %param.13) | copy-start | bytes 98308
  105.6 146.1 %copy-start.3 = (f32[1,64,128]{2,1,0:T(8,128)S(1)}, f32[1,64,128]{2,1,0:T(8,128)}, u32[]{:S(2)}) copy-start(f32[1,64,128]{2,1,0:T(8,128)} %param.15) | copy-start | bytes 98308
  105.6 146.1 %copy-start.4 = (f32[1,64,128]{2,1,0:T(8,128)S(1)}, f32[1,64,128]{2,1,0:T(8,128)}, u32[]{:S(2)}) copy-start(f32[1,64,128]{2,1,0:T(8,128)} %param.16) | copy-start | bytes 98308
  105.6 146.1 %copy-start.5 = (f32[64,128]{1,0:T(8,128)S(1)}, f32[64,128]{1,0:T(8,128)}, u32[]{:S(2)}) copy-start(f32[64,128]{1,0:T(8,128)} %param.21) | copy-start | bytes 98308
  105.6 146.1 %copy-start.7 = (f32[1,64]{1,0:T(1,128)S(1)}, f32[1,64]{1,0:T(1,128)}, u32[]{:S(2)}) copy-start(f32[1,64]{1,0:T(1,128)} %param.14) | copy-start | bytes 772
  105.6 147.6 %copy-start.8 = (f32[1,64]{1,0:T(1,128)S(1)}, f32[1,64]{1,0:T(1,128)}, u32[]{:S(2)}) copy-start(f32[1,64]{1,0:T(1,128)} %param.18) | copy-start | bytes 772
  105.6 147.6 %copy-start.9 = (f32[1,64]{1,0:T(1,128)S(1)}, f32[1,64]{1,0:T(1,128)}, u32[]{:S(2)}) copy-start(f32[1,64]{1,0:T(1,128)} %param.17) | copy-start | bytes 772
Sparse Core Ops, SparseCore 0:
  11.9 88.9 all-gather.1
  109.2 142.4 reduce-scatter.1
where the time goes:
time: 265 us; the launch traced here: 261 us
  waiting for transfers between devices  205 us (77%)
  blocking collectives  26.3 us (10%)
  between operations  14.2 us (5%)
  matrix products  7.95 us (3%)
  other arithmetic  6.66 us (3%)
    reduce_scatter x1, waiting for transfers between devices, per_device(): lax.psum_scatter(lax.dot_general(columns, error, contract, preferred_elem...  116 us
    all_gather x1, waiting for transfers between devices, per_device(): lax.all_gather(effective, 'fsdp', axis=0, tiled=True)  89.1 us
    psum x1, blocking collectives, per_device(): delta_sum = lax.psum(delta, 'island').astype(jnp.float32)  26.3 us
  transfers between devices with their start and end apart: 2, of which 2 were waited for; matrix products, arithmetic and copies ran while one was open for 1% of the time, Pallas kernels for 0%

commit v1 on v0

v1 whole, which is shorter than its diff:
```python
import functools

import jax
import jax.numpy as jnp
from jax import lax
from jax.experimental import pallas as pl
from jax.experimental.pallas import tpu as pltpu
from jax.sharding import PartitionSpec as P

MESH = pl.DeviceIdType.MESH
NZ, NY, NC = 8, 4, 2
F32, BF16 = jnp.float32, jnp.bfloat16


def ring_order(n):
    return sorted(range(1, n), key=lambda d: (min(d, n - d), d))


def adamw(param, grad, first, second):
    first_next = 0.9 * first + 0.1 * grad
    second_next = 0.95 * second + 0.05 * grad * grad
    inner = param - 0.01 * (first_next / (jnp.sqrt(second_next) + 1e-08) + 0.1 * param)
    return inner, first_next, second_next


def kernel(
    nz,
    ny,
    ni,
    tokens_hbm,
    target_hbm,
    weight_hbm,
    gain_ref,
    first_w_hbm,
    second_w_hbm,
    first_g_ref,
    second_g_ref,
    anchor_hbm,
    snapshot_hbm,
    momentum_hbm,
    values_ref,
    weight_new_ref,
    gain_new_ref,
    first_w_ref,
    second_w_ref,
    first_g_out,
    second_g_out,
    anchor_new_ref,
    momentum_new_ref,
    tok,
    tok_t,
    target,
    weight,
    first_w,
    second_w,
    anchor,
    snapshot,
    momentum,
    own,
    eff,
    squares,
    acc,
    err,
    delta,
    mine,
    give,
    take,
    part,
    recv_a,
    recv_b,
    sum_a,
    sum_b,
    send_a,
    send_b,
    last_a,
    last_b,
    summed,
    load_sem,
    tok_sem,
    send_sem,
    sib_sem,
    y_a_sem,
    z_b_sem,
    a_sem,
    b_sem,
    delta_sem,
    pair_sem,
    ra_sem,
    rb_sem,
    la_sem,
    lb_sem,
):
    f = lax.axis_index("fsdp")
    isl = lax.axis_index("island")
    z, y, c = f // (ny * NC), (f // NC) % ny, f % NC
    rows, head = own.shape
    half = rows // 2
    tall = tok.shape[0]
    width = ny * NC * rows
    dim = tok.shape[1]
    up, low = pl.ds(0, half), pl.ds(half, half)
    near_z, near_y = ring_order(nz), ring_order(ny)
    far_z, far_y = near_z[::-1], near_y[::-1]

    def at_z(d):
        return lax.rem(z + d, nz)

    def at_y(d):
        return lax.rem(y + d, ny)

    def to_z(d):
        return {"island": isl, "fsdp": (at_z(d) * ny + y) * NC + c}

    def to_y(d):
        return {"island": isl, "fsdp": (z * ny + at_y(d)) * NC + c}

    sibling = {"island": isl, "fsdp": (z * ny + y) * NC + 1 - c}

    def to_isl(d):
        return {"island": lax.rem(isl + d, ni), "fsdp": f}

    barrier = pltpu.get_barrier_semaphore()
    partners = [to_z(d) for d in far_z] + [to_y(d) for d in far_y] + [to_isl(d) for d in range(1, ni)] + [sibling]
    for partner in partners:
        pl.semaphore_signal(barrier, inc=1, device_id=partner, device_id_type=MESH)

    loads = [
        pltpu.make_async_copy(src, dst, load_sem.at[n])
        for n, (src, dst) in enumerate(
            [
                (weight_hbm.at[0], weight),
                (anchor_hbm, anchor),
                (snapshot_hbm.at[0], snapshot),
                (target_hbm, target),
                (first_w_hbm.at[0], first_w),
                (second_w_hbm.at[0], second_w),
                (momentum_hbm, momentum),
            ]
        )
    ]
    loads[0].start()
    for k in range(nz):
        cols = pl.ds(k * width, width)
        pltpu.make_async_copy(tokens_hbm.at[:, cols], tok.at[:, cols], tok_sem.at[k]).start()
    for load in loads[1:]:
        load.start()

    eye = lax.broadcasted_iota(jnp.int32, (rows, rows), 0) == lax.broadcasted_iota(jnp.int32, (rows, rows), 1)

    def as_column(row):
        return jnp.sum(jnp.where(eye, jnp.broadcast_to(row, (rows, rows)), 0.0), axis=1, keepdims=True)

    def as_row(column):
        return jnp.sum(jnp.where(eye, jnp.broadcast_to(column, (rows, rows)), 0.0), axis=0, keepdims=True)

    scale = 1.0 / float(dim) ** 0.5
    gain = as_column(gain_ref[...])
    loads[0].wait()
    own[...] = (gain * weight[...] * scale).astype(BF16)
    eff[z, y, c] = own[...]
    squares[...] = jnp.zeros_like(squares)

    def prepare(k, carry):
        cols = pl.ds(pl.multiple_of(k * width, width), width)
        pltpu.make_async_copy(tokens_hbm.at[:, cols], tok.at[:, cols], tok_sem.at[k]).wait()
        x = tok[:, cols]
        tok_t[cols, :] = x.T
        wide = x.astype(F32)
        total = squares[...]
        for j in range(width // head):
            piece = wide[:, j * head : (j + 1) * head]
            total = total + piece * piece
        squares[...] = total
        return carry

    lax.fori_loop(0, nz // 2, prepare, 0)

    sent = []

    def send(src, dst, sem, device):
        copy = pltpu.make_async_remote_copy(
            src_ref=src,
            dst_ref=dst,
            send_sem=send_sem.at[len(sent)],
            recv_sem=sem,
            device_id=device,
            device_id_type=MESH,
        )
        copy.start()
        sent.append(copy)

    def arrived(ref, sem):
        pltpu.make_async_copy(ref, ref, sem).wait()

    pl.semaphore_wait(barrier, len(partners))

    mine_up, mine_low = eff.at[z, y, c, up], eff.at[z, y, c, low]
    for d in far_y:
        send(own.at[up], mine_up, y_a_sem.at[y], to_y(d))
    for d in far_z:
        send(own.at[low], mine_low, z_b_sem.at[z], to_z(d))
    for d in far_z:
        send(own.at[up], mine_up, a_sem.at[z], to_z(d))
    for d in far_y:
        send(own.at[low], mine_low, b_sem.at[z], to_y(d))

    lax.fori_loop(nz // 2, nz, prepare, 0)

    def pass_up(d):
        block = eff.at[z, at_y(d), c, up]
        arrived(block, y_a_sem.at[at_y(d)])
        for e in far_z:
            send(block, block, a_sem.at[z], to_z(e))

    def pass_low(d):
        block = eff.at[at_z(d), y, c, low]
        arrived(block, z_b_sem.at[at_z(d)])
        for e in far_y:
            send(block, block, b_sem.at[at_z(d)], to_y(e))

    y_left, z_left = list(near_y), list(near_z)
    while y_left or z_left:
        for _ in range(2):
            if z_left:
                pass_low(z_left.pop(0))
        if y_left:
            pass_up(y_left.pop(0))

    mean_sq = jnp.sum(squares[...], axis=1, keepdims=True) / float(dim)
    rstd = lax.rsqrt(mean_sq + 1e-05)

    order = [0] + near_z

    def hand_over(n):
        zb = at_z(order[n])
        if n:
            arrived(eff.at[zb, :, c, up], a_sem.at[zb])
        arrived(eff.at[zb, pl.ds(0, ny - 1), c, low], b_sem.at[zb])
        block = eff.at[zb, :, c]
        send(block, block, sib_sem.at[n], sibling)

    def multiply(n):
        zb = at_z(order[n])
        arrived(eff.at[zb, :, 1 - c], sib_sem.at[n])
        cols = pl.ds(pl.multiple_of(zb * width, width), width)
        product = jnp.dot(tok[:, cols], eff[zb].reshape(width, head), preferred_element_type=F32)
        if n:
            acc[...] += product
        else:
            acc[...] = product

    for n in range(nz):
        hand_over(n)
        if n:
            multiply(n - 1)
    multiply(nz - 1)

    loads[3].wait()
    projected = acc[...] * rstd
    values_ref[...] = projected.astype(BF16)
    err[...] = ((projected - target[...].astype(F32)) * rstd).astype(BF16)

    back = far_z + [0]

    def terms(n):
        zb = at_z(back[n])
        cols = pl.ds(pl.multiple_of(zb * width, width), width)
        block = jnp.dot(tok_t[cols, :], err[...], preferred_element_type=F32).reshape(ny, NC, rows, head)
        first, second = block[:, 0], block[:, 1]
        mine[n] = jnp.where(c == 0, first, second)
        give[n] = jnp.where(c == 0, second, first).astype(BF16)
        send(give.at[n], take.at[n], pair_sem.at[n], sibling)

    def add_pair(n):
        arrived(take.at[n], pair_sem.at[n])
        part[n] = (mine[n] + take[n].astype(F32)).astype(BF16)
        if back[n]:
            send(part.at[n, :, up], recv_a.at[z], ra_sem.at[z], to_z(back[n]))

    group = nz // 2

    def send_low(g):
        span = pl.ds(g * group, group)
        for d in far_y:
            send(part.at[span, at_y(d), low], recv_b.at[y, span], rb_sem.at[g, y], to_y(d))

    lag = 2
    for n in range(nz + lag):
        if n < nz:
            terms(n)
        if n >= lag:
            add_pair(n - lag)
            if (n - lag + 1) % group == 0:
                send_low((n - lag) // group)

    loads[1].wait()
    loads[2].wait()
    delta[isl] = (anchor[...] - snapshot[...]).astype(BF16)
    for d in range(1, ni):
        send(delta.at[isl], delta.at[isl], delta_sem.at[isl], to_isl(d))

    def low_sums(g):
        span = pl.ds(g * group, group)
        total = part[span, y, low].astype(F32)
        for d in near_y:
            arrived(recv_b.at[at_y(d), span], rb_sem.at[g, at_y(d)])
            total = total + recv_b[at_y(d), span].astype(F32)
        sum_b[span] = total
        send_b[span] = total.astype(BF16)
        for n in range(g * group, (g + 1) * group):
            if back[n]:
                send(send_b.at[n], last_b.at[z], lb_sem.at[z], to_z(back[n]))

    low_sums(0)
    total = part[nz - 1, :, up].astype(F32)
    for d in near_z:
        arrived(recv_a.at[at_z(d)], ra_sem.at[at_z(d)])
        total = total + recv_a[at_z(d)].astype(F32)
    sum_a[...] = total
    send_a[...] = total.astype(BF16)
    for d in far_y:
        send(send_a.at[at_y(d)], last_a.at[y], la_sem.at[y], to_y(d))
    low_sums(1)

    loads[6].wait()
    for d in range(1, ni):
        there = lax.rem(isl + d, ni)
        arrived(delta.at[there], delta_sem.at[there])
    delta_sum = delta[0].astype(F32)
    for n in range(1, ni):
        delta_sum = delta_sum + delta[n].astype(F32)
    mean_delta = delta_sum / float(ni)
    momentum_next = 0.9 * momentum[...] + mean_delta
    anchor_next = anchor[...] - 0.7 * (mean_delta + 0.9 * momentum_next)
    momentum_new_ref[...] = momentum_next
    anchor_new_ref[...] = anchor_next

    total = sum_a[y]
    for d in near_y:
        arrived(last_a.at[at_y(d)], la_sem.at[at_y(d)])
        total = total + last_a[at_y(d)].astype(F32)
    summed[up, :] = total
    total = sum_b[nz - 1]
    for d in near_z:
        arrived(last_b.at[at_z(d)], lb_sem.at[at_z(d)])
        total = total + last_b[at_z(d)].astype(F32)
    summed[low, :] = total

    loads[4].wait()
    loads[5].wait()
    grad = summed[...]
    grad_gain = as_row(jnp.sum(weight[...] * grad, axis=1, keepdims=True)) * scale
    inner, first_next, second_next = adamw(weight[...], gain * grad * scale, first_w[...], second_w[...])
    weight_new_ref[0] = 0.5 * inner + 0.5 * anchor_next
    first_w_ref[0] = first_next
    second_w_ref[0] = second_next
    inner, first_next, second_next = adamw(gain_ref[...], grad_gain, first_g_ref[...], second_g_ref[...])
    gain_new_ref[...] = inner
    first_g_out[...] = first_next
    second_g_out[...] = second_next
    for copy in sent:
        copy.wait_send()


def per_device(nz, ny, ni, *args):
    tokens, target, weight = args[:3]
    tall, dim = tokens.shape
    _, rows, head = weight.shape
    half = rows // 2
    vmem = pl.BlockSpec(memory_space=pltpu.VMEM)
    hbm = pl.BlockSpec(memory_space=pl.ANY)
    shard, line = (1, rows, head), (1, rows)
    outs = [
        ((tall, head), BF16),
        (shard, F32),
        (line, F32),
        (shard, F32),
        (shard, F32),
        (line, F32),
        (line, F32),
        ((rows, head), F32),
        ((rows, head), F32),
    ]
    dma = pltpu.SemaphoreType.DMA
    sends = 2 * (nz - 1 + ny - 1) + 2 * (nz - 1) * (ny - 1) + nz
    sends += nz + (nz - 1) + 2 * (ny - 1) + (ni - 1) + (nz - 1) + (ny - 1)
    blocks = (nz, ny, rows, head)
    scratch = [
        pltpu.VMEM((tall, dim), BF16),
        pltpu.VMEM((dim, tall), BF16),
        pltpu.VMEM((tall, head), BF16),
        *[pltpu.VMEM((rows, head), F32) for _ in range(6)],
        pltpu.VMEM((rows, head), BF16),
        pltpu.VMEM((nz, ny, NC, rows, head), BF16),
        pltpu.VMEM((tall, head), F32),
        pltpu.VMEM((tall, head), F32),
        pltpu.VMEM((tall, head), BF16),
        pltpu.VMEM((ni, rows, head), BF16),
        pltpu.VMEM(blocks, F32),
        pltpu.VMEM(blocks, BF16),
        pltpu.VMEM(blocks, BF16),
        pltpu.VMEM(blocks, BF16),
        pltpu.VMEM((nz, ny, half, head), BF16),
        pltpu.VMEM((ny, nz, half, head), BF16),
        pltpu.VMEM((ny, half, head), F32),
        pltpu.VMEM((nz, half, head), F32),
        pltpu.VMEM((ny, half, head), BF16),
        pltpu.VMEM((nz, half, head), BF16),
        pltpu.VMEM((ny, half, head), BF16),
        pltpu.VMEM((nz, half, head), BF16),
        pltpu.VMEM((rows, head), F32),
        dma((7,)),
        dma((nz,)),
        dma((sends,)),
        dma((nz,)),
        dma((ny,)),
        dma((nz,)),
        dma((nz,)),
        dma((nz,)),
        dma((ni,)),
        dma((nz,)),
        dma((nz,)),
        dma((2, ny)),
        dma((ny,)),
        dma((nz,)),
    ]
    return pl.pallas_call(
        functools.partial(kernel, nz, ny, ni),
        out_shape=[jax.ShapeDtypeStruct(s, t) for s, t in outs],
        in_specs=[hbm, hbm, hbm, vmem, hbm, hbm, vmem, vmem, hbm, hbm, hbm],
        out_specs=[vmem] * len(outs),
        scratch_shapes=scratch,
        compiler_params=pltpu.CompilerParams(
            collective_id=0, has_side_effects=True, vmem_limit_bytes=40 * 2**20
        ),
        name="diloco_step",
    )(*args)


def solution(mesh, nz=NZ, ny=NY):
    rows = P(("island", "fsdp"), None)
    shard = P("island", "fsdp", None)
    line = P("island", "fsdp")
    whole = P("fsdp", None)
    return jax.shard_map(
        functools.partial(per_device, nz, ny, mesh.shape["island"]),
        mesh=mesh,
        in_specs=(rows, rows, shard, line, shard, shard, line, line, whole, shard, whole),
        out_specs=(rows, shard, line, shard, shard, line, line, whole, whole),
        check_vma=False,
    )
```

time: 265 us -> 61.6 us (0.23); the launches traced: 261 us -> 60.9 us
  waiting for transfers between devices: 205 us -> 0 us
  Pallas kernels: 0 us -> 45.4 us
  blocking collectives: 26.3 us -> 0 us
  local copies, waits for them, and re-layouts: 0.06 us -> 14.9 us
  between operations: 14.2 us -> 0.68 us
  matrix products: 7.95 us -> 0 us
  other arithmetic: 6.66 us -> 0 us
    reduce_scatter x1 -> x0, waiting for transfers between devices: 116 us -> none  [per_device(): lax.psum_scatter(lax.dot_general(columns, error, contract, preferred_elem...]
    all_gather x1 -> x0, waiting for transfers between devices: 89.1 us -> none  [per_device(): lax.all_gather(effective, 'fsdp', axis=0, tiled=True)]
    pallas_call x0 -> x1, Pallas kernels: none -> 45.4 us  [per_device(): pl.pallas_call(functools.partial(kernel, nz, ny, ni), out_shape=[jax.Shap...]
    psum x1 -> x0, blocking collectives: 26.3 us -> none  [per_device(): delta_sum = lax.psum(delta, 'island').astype(jnp.float32)]
    unnamed x22 -> x31, local copies, waits for them, and re-layouts: 0.06 us -> 14.9 us
    dot_general x2 -> x0, matrix products: 7.95 us -> none  [the longest x1 4.59 us: per_device(): jnp.dot(columns, lax.all_gather(effective, 'fsdp', axis=0, tiled=True), p...]
    reduce_sum x1 -> x0, other arithmetic: 3.08 us -> none  [per_device(): rstd = lax.rsqrt(jnp.mean(wide * wide, axis=1, keepdims=True) + 1e-05)]
  transfers between devices with their start and end apart: 2 -> 0, of which waited for: 2 -> 0; matrix products, arithmetic and copies ran while one was open for 1% -> 0% of each run, Pallas kernels for 0% -> 0%
where the time goes in v1:
time: 61.6 us; the launch traced here: 60.9 us
  Pallas kernels  45.4 us (74%)
  local copies, waits for them, and re-layouts  14.9 us (24%)
  between operations  0.68 us (1%)
    pallas_call x1, Pallas kernels, per_device(): pl.pallas_call(functools.partial(kernel, nz, ny, ni), out_shape=[jax.Shap...  45.4 us
    unnamed x31, local copies, waits for them, and re-layouts  14.9 us

profile of v1, /device:TPU:1, one launch (start us, length us, event | category | flops | bytes accessed | tf_op | source)
XLA Modules:
  0.0 60.9 jit_solution(17868185899645743393)
XLA Ops:
  0.6 0.0 copy-start
  0.7 2.2 %copy-done = bf16[512,4096]{1,0:T(8,128)(2,1)S(1)} copy-done((bf16[512,4096]{1,0:T(8,128)(2,1)S(1)}, bf16[512,4096]{1,0:T(8,128)(2,1)}, u32[]{:S(2)}) %copy-start) | copy-done | bytes 4194328
  2.8 0.0 copy-start.1
  2.8 0.9 %copy-done.1 = bf16[512,128]{1,0:T(8,128)(2,1)S(1)} copy-done((bf16[512,128]{1,0:T(8,128)(2,1)S(1)}, bf16[512,128]{1,0:T(8,128)(2,1)}, u32[]{:S(2)}) %copy-start.1) | copy-done | bytes 131096
  3.7 0.0 copy-start.2
  3.7 0.8 %copy-done.2 = f32[1,64,128]{2,1,0:T(8,128)S(1)} copy-done((f32[1,64,128]{2,1,0:T(8,128)S(1)}, f32[1,64,128]{2,1,0:T(8,128)}, u32[]{:S(2)}) %copy-start.2) | copy-done | bytes 32792
  4.5 0.0 copy-start.3
  4.5 0.8 %copy-done.3 = f32[1,64,128]{2,1,0:T(8,128)S(1)} copy-done((f32[1,64,128]{2,1,0:T(8,128)S(1)}, f32[1,64,128]{2,1,0:T(8,128)}, u32[]{:S(2)}) %copy-start.3) | copy-done | bytes 32792
  5.3 0.0 copy-start.4
  5.3 0.8 %copy-done.4 = f32[1,64,128]{2,1,0:T(8,128)S(1)} copy-done((f32[1,64,128]{2,1,0:T(8,128)S(1)}, f32[1,64,128]{2,1,0:T(8,128)}, u32[]{:S(2)}) %copy-start.4) | copy-done | bytes 32792
  6.0 0.0 copy-start.5
  6.0 0.8 %copy-done.5 = f32[64,128]{1,0:T(8,128)S(1)} copy-done((f32[64,128]{1,0:T(8,128)S(1)}, f32[64,128]{1,0:T(8,128)}, u32[]{:S(2)}) %copy-start.5) | copy-done | bytes 32792
  6.8 0.0 copy-start.6
  6.8 0.8 %copy-done.6 = f32[1,64,128]{2,1,0:T(8,128)S(1)} copy-done((f32[1,64,128]{2,1,0:T(8,128)S(1)}, f32[1,64,128]{2,1,0:T(8,128)}, u32[]{:S(2)}) %copy-start.6) | copy-done | bytes 32792
  7.5 0.0 copy-start.7
  7.5 0.8 %copy-done.7 = f32[64,128]{1,0:T(8,128)S(1)} copy-done((f32[64,128]{1,0:T(8,128)S(1)}, f32[64,128]{1,0:T(8,128)}, u32[]{:S(2)}) %copy-start.7) | copy-done | bytes 32792
  8.3 0.0 copy-start.8
  8.3 0.7 %copy-done.8 = f32[1,64]{1,0:T(1,128)S(1)} copy-done((f32[1,64]{1,0:T(1,128)S(1)}, f32[1,64]{1,0:T(1,128)}, u32[]{:S(2)}) %copy-start.8) | copy-done | bytes 280
  8.9 0.0 copy-start.9
  8.9 0.7 %copy-done.9 = f32[1,64]{1,0:T(1,128)S(1)} copy-done((f32[1,64]{1,0:T(1,128)S(1)}, f32[1,64]{1,0:T(1,128)}, u32[]{:S(2)}) %copy-start.9) | copy-done | bytes 280
  9.6 0.0 copy-start.10
  9.6 0.7 %copy-done.10 = f32[1,64]{1,0:T(1,128)S(1)} copy-done((f32[1,64]{1,0:T(1,128)S(1)}, f32[1,64]{1,0:T(1,128)}, u32[]{:S(2)}) %copy-start.10) | copy-done | bytes 280
  10.3 45.4 %diloco_step.1 = (bf16[512,128]{1,0:T(8,128)(2,1)S(1)}, f32[1,64,128]{2,1,0:T(8,128)S(1)}, f32[1,64]{1,0:T(1,128)S(1)}, f32[1,64,128]{2,1,0:T(8,128)S(1)}, f32[1...) custom-call(bf16[512,4096]{1,0:T(8,128)(2,1)S(1)} %copy-done, ...), custom_call_target="tpu_custom_call" | custom-call | tf_op jit(solution)/shard_map/diloco_step/pallas_call | solution.py:427
  55.6 0.7 %copy.29 = bf16[512,128]{1,0:T(8,128)(2,1)} copy(bf16[512,128]{1,0:T(8,128)(2,1)S(1)} %get-tuple-element.18) | data formatting | bytes 262144
  56.3 0.6 %copy.30 = f32[1,64,128]{2,1,0:T(8,128)} copy(f32[1,64,128]{2,1,0:T(8,128)S(1)} %get-tuple-element.19) | data formatting | bytes 65536
  56.9 0.5 copy.31
  57.4 0.6 %copy.32 = f32[1,64,128]{2,1,0:T(8,128)} copy(f32[1,64,128]{2,1,0:T(8,128)S(1)} %get-tuple-element.21) | data formatting | bytes 65536
  58.0 0.6 %copy.33 = f32[1,64,128]{2,1,0:T(8,128)} copy(f32[1,64,128]{2,1,0:T(8,128)S(1)} %get-tuple-element.22) | data formatting | bytes 65536
  58.6 0.5 copy.34
  59.2 0.5 copy.35
  59.7 0.6 %copy.36 = f32[64,128]{1,0:T(8,128)} copy(f32[64,128]{1,0:T(8,128)S(1)} %get-tuple-element.25) | data formatting | bytes 65536
  60.3 0.6 %copy.37 = f32[64,128]{1,0:T(8,128)} copy(f32[64,128]{1,0:T(8,128)S(1)} %get-tuple-element.26) | data formatting | bytes 65536
Async XLA Ops:
  0.6 2.2 %copy-start = (bf16[512,4096]{1,0:T(8,128)(2,1)S(1)}, bf16[512,4096]{1,0:T(8,128)(2,1)}, u32[]{:S(2)}) copy-start(bf16[512,4096]{1,0:T(8,128)(2,1)} %tokens_hbm.1) | copy-start | bytes 12582916
  2.8 0.9 %copy-start.1 = (bf16[512,128]{1,0:T(8,128)(2,1)S(1)}, bf16[512,128]{1,0:T(8,128)(2,1)}, u32[]{:S(2)}) copy-start(bf16[512,128]{1,0:T(8,128)(2,1)} %target_hbm.1) | copy-start | bytes 393220
  3.7 0.8 %copy-start.2 = (f32[1,64,128]{2,1,0:T(8,128)S(1)}, f32[1,64,128]{2,1,0:T(8,128)}, u32[]{:S(2)}) copy-start(f32[1,64,128]{2,1,0:T(8,128)} %weight_hbm.1) | copy-start | bytes 98308
  4.5 0.8 %copy-start.3 = (f32[1,64,128]{2,1,0:T(8,128)S(1)}, f32[1,64,128]{2,1,0:T(8,128)}, u32[]{:S(2)}) copy-start(f32[1,64,128]{2,1,0:T(8,128)} %first_w_hbm.1) | copy-start | bytes 98308
  5.3 0.8 %copy-start.4 = (f32[1,64,128]{2,1,0:T(8,128)S(1)}, f32[1,64,128]{2,1,0:T(8,128)}, u32[]{:S(2)}) copy-start(f32[1,64,128]{2,1,0:T(8,128)} %second_w_hbm.1) | copy-start | bytes 98308
  6.0 0.8 %copy-start.5 = (f32[64,128]{1,0:T(8,128)S(1)}, f32[64,128]{1,0:T(8,128)}, u32[]{:S(2)}) copy-start(f32[64,128]{1,0:T(8,128)} %anchor_hbm.1) | copy-start | bytes 98308
  6.8 0.8 %copy-start.6 = (f32[1,64,128]{2,1,0:T(8,128)S(1)}, f32[1,64,128]{2,1,0:T(8,128)}, u32[]{:S(2)}) copy-start(f32[1,64,128]{2,1,0:T(8,128)} %snapshot_hbm.1) | copy-start | bytes 98308
  7.5 0.8 %copy-start.7 = (f32[64,128]{1,0:T(8,128)S(1)}, f32[64,128]{1,0:T(8,128)}, u32[]{:S(2)}) copy-start(f32[64,128]{1,0:T(8,128)} %momentum_hbm.1) | copy-start | bytes 98308
  8.3 0.7 %copy-start.8 = (f32[1,64]{1,0:T(1,128)S(1)}, f32[1,64]{1,0:T(1,128)}, u32[]{:S(2)}) copy-start(f32[1,64]{1,0:T(1,128)} %gain_ref.1) | copy-start | bytes 772
  8.9 0.7 %copy-start.9 = (f32[1,64]{1,0:T(1,128)S(1)}, f32[1,64]{1,0:T(1,128)}, u32[]{:S(2)}) copy-start(f32[1,64]{1,0:T(1,128)} %first_g_ref.1) | copy-start | bytes 772
  9.6 0.7 %copy-start.10 = (f32[1,64]{1,0:T(1,128)S(1)}, f32[1,64]{1,0:T(1,128)}, u32[]{:S(2)}) copy-start(f32[1,64]{1,0:T(1,128)} %second_g_ref.1) | copy-start | bytes 772

commit v2 on v1

v2 whole, which is shorter than its diff:
```python
import functools

import jax
import jax.numpy as jnp
from jax import lax
from jax.experimental import pallas as pl
from jax.experimental.pallas import tpu as pltpu
from jax.sharding import PartitionSpec as P

MESH = pl.DeviceIdType.MESH
NZ, NY, NC = 8, 4, 2
F32, BF16 = jnp.float32, jnp.bfloat16
PREPARED = {1: 5, 2: 7, 3: 8}


def ring_order(n):
    return sorted(range(1, n), key=lambda d: (min(d, n - d), d))


def adamw(param, grad, first, second):
    first_next = 0.9 * first + 0.1 * grad
    second_next = 0.95 * second + 0.05 * grad * grad
    inner = param - 0.01 * (first_next / (jnp.sqrt(second_next) + 1e-08) + 0.1 * param)
    return inner, first_next, second_next


def eye(n):
    return lax.broadcasted_iota(jnp.int32, (n, n), 0) == lax.broadcasted_iota(jnp.int32, (n, n), 1)


def as_column(row):
    n = row.shape[1]
    return jnp.sum(jnp.where(eye(n), jnp.broadcast_to(row, (n, n)), 0.0), axis=1, keepdims=True)


def as_row(column):
    n = column.shape[0]
    return jnp.sum(jnp.where(eye(n), jnp.broadcast_to(column, (n, n)), 0.0), axis=0, keepdims=True)


def exchange(
    nz,
    ny,
    ni,
    tokens_hbm,
    target_hbm,
    weight_hbm,
    gain_hbm,
    anchor_hbm,
    snapshot_hbm,
    momentum_hbm,
    values_ref,
    summed,
    anchor_new_ref,
    momentum_new_ref,
    tok,
    tok_t,
    target,
    weight,
    anchor,
    snapshot,
    momentum,
    gain_row,
    own,
    eff,
    squares,
    acc,
    err,
    delta,
    mine,
    give,
    take,
    part,
    recv_a,
    recv_b,
    send_a,
    send_b,
    last_a,
    last_b,
    load_sem,
    tok_sem,
    send_sem,
    sib_sem,
    y_a_sem,
    z_b_sem,
    a_sem,
    b_sem,
    delta_sem,
    pair_sem,
    ra_sem,
    rb_sem,
    la_sem,
    lb_sem,
):
    f = lax.axis_index("fsdp")
    isl = lax.axis_index("island")
    z, y, c = f // (ny * NC), (f // NC) % ny, f % NC
    rows, head = own.shape
    half = rows // 2
    tall = tok.shape[0]
    width = ny * NC * rows
    dim = tok.shape[1]
    up, low = pl.ds(0, half), pl.ds(half, half)
    near_z, near_y = ring_order(nz), ring_order(ny)
    far_z = near_z[::-1]

    def at_z(d):
        return lax.rem(z + d, nz)

    def at_y(d):
        return lax.rem(y + d, ny)

    def to_z(d):
        return {"island": isl, "fsdp": (at_z(d) * ny + y) * NC + c}

    def to_y(d):
        return {"island": isl, "fsdp": (z * ny + at_y(d)) * NC + c}

    sibling = {"island": isl, "fsdp": (z * ny + y) * NC + 1 - c}

    def to_isl(d):
        return {"island": lax.rem(isl + d, ni), "fsdp": f}

    barrier = pltpu.get_barrier_semaphore()
    partners = [to_z(d) for d in far_z] + [to_y(d) for d in near_y] + [to_isl(d) for d in range(1, ni)] + [sibling]
    for partner in partners:
        pl.semaphore_signal(barrier, inc=1, device_id=partner, device_id_type=MESH)

    loads = [
        pltpu.make_async_copy(src, dst, load_sem.at[n])
        for n, (src, dst) in enumerate(
            [
                (weight_hbm.at[0], weight),
                (anchor_hbm, anchor),
                (snapshot_hbm.at[0], snapshot),
                (target_hbm, target),
                (momentum_hbm, momentum),
                (gain_hbm, gain_row),
            ]
        )
    ]
    loads[5].start()
    loads[0].start()
    for k in range(nz):
        cols = pl.ds(k * width, width)
        pltpu.make_async_copy(tokens_hbm.at[:, cols], tok.at[:, cols], tok_sem.at[k]).start()
    for load in loads[1:5]:
        load.start()

    scale = 1.0 / float(dim) ** 0.5
    loads[5].wait()
    gain = as_column(gain_row[...])
    loads[0].wait()
    own[...] = (gain * weight[...] * scale).astype(BF16)
    eff[z, y, c] = own[...]
    squares[...] = jnp.zeros_like(squares)

    def prepare(k, carry):
        cols = pl.ds(pl.multiple_of(k * width, width), width)
        pltpu.make_async_copy(tokens_hbm.at[:, cols], tok.at[:, cols], tok_sem.at[k]).wait()
        x = tok[:, cols]
        tok_t[k] = x.T.reshape(ny, NC, 2, half, tall)
        wide = x.astype(F32)
        total = squares[...]
        for j in range(width // head):
            piece = wide[:, j * head : (j + 1) * head]
            total = total + piece * piece
        squares[...] = total
        return carry

    sent = []

    def send(src, dst, sem, device):
        copy = pltpu.make_async_remote_copy(
            src_ref=src,
            dst_ref=dst,
            send_sem=send_sem.at[len(sent)],
            recv_sem=sem,
            device_id=device,
            device_id_type=MESH,
        )
        copy.start()
        sent.append(copy)

    def arrived(ref, sem):
        pltpu.make_async_copy(ref, ref, sem).wait()

    pl.semaphore_wait(barrier, len(partners))

    mine_up, mine_low = eff.at[z, y, c, up], eff.at[z, y, c, low]
    for d in near_z:
        send(own.at[low], mine_low, z_b_sem.at[z], to_z(d))
    for d in near_y:
        send(own.at[up], mine_up, y_a_sem.at[y], to_y(d))

    def pass_up(d):
        block = eff.at[z, at_y(d), c, up]
        arrived(block, y_a_sem.at[at_y(d)])
        for e in near_z:
            send(block, block, a_sem.at[z], to_z(e))

    def pass_low(d):
        block = eff.at[at_z(d), y, c, low]
        arrived(block, z_b_sem.at[at_z(d)])
        for e in near_y:
            send(block, block, b_sem.at[at_z(d)], to_y(e))

    for d in near_z:
        send(own.at[up], mine_up, a_sem.at[z], to_z(d))
    for d in near_y:
        send(own.at[low], mine_low, b_sem.at[z], to_y(d))

    hops = [(min(d, nz - d), pass_low, d) for d in near_z] + [(2 * min(d, ny - d), pass_up, d) for d in near_y]
    hops.sort(key=lambda step: step[0])
    ready = 0
    for links, step, d in hops:
        if links in PREPARED and ready < min(PREPARED[links], nz):
            lax.fori_loop(ready, min(PREPARED[links], nz), prepare, 0)
            ready = min(PREPARED[links], nz)
        step(d)
    lax.fori_loop(ready, nz, prepare, 0)

    mean_sq = jnp.sum(squares[...], axis=1, keepdims=True) / float(dim)
    rstd = lax.rsqrt(mean_sq + 1e-05)

    order = [0] + near_z

    def hand_over(n):
        zb = at_z(order[n])
        if n:
            arrived(eff.at[zb, :, c, up], a_sem.at[zb])
        arrived(eff.at[zb, pl.ds(0, ny - 1), c, low], b_sem.at[zb])
        block = eff.at[zb, :, c]
        send(block, block, sib_sem.at[n], sibling)

    def multiply(n):
        zb = at_z(order[n])
        arrived(eff.at[zb, :, 1 - c], sib_sem.at[n])
        cols = pl.ds(pl.multiple_of(zb * width, width), width)
        product = jnp.dot(tok[:, cols], eff[zb].reshape(width, head), preferred_element_type=F32)
        if n:
            acc[...] += product
        else:
            acc[...] = product

    for n in range(nz):
        hand_over(n)
        if n:
            multiply(n - 1)
    multiply(nz - 1)

    loads[3].wait()
    projected = acc[...] * rstd
    values_ref[...] = projected.astype(BF16)
    err[...] = ((projected - target[...].astype(F32)) * rstd).astype(BF16)

    back_y, back_z = near_y[::-1] + [0], far_z + [0]
    pairs = [back_z[n : n + 2] for n in range(0, nz, 2)]
    groups = [g for up_down in zip(range(ny), range(ny)) for g in (("up", up_down[0]), ("low", up_down[1]))]

    def product(lhs):
        return jnp.dot(lhs, err[...], preferred_element_type=F32).reshape(-1, NC, half, head)

    def terms(g):
        kind, n = groups[g]
        if kind == "up":
            block = product(tok_t[:, at_y(back_y[n]), :, 0].reshape(nz * NC * half, tall))
            first, second = block[:, 0], block[:, 1]
            mine[g] = jnp.where(c == 0, first, second)
            give[g] = jnp.where(c == 0, second, first).astype(BF16)
        else:
            for m, d in enumerate(pairs[n]):
                block = product(tok_t[at_z(d), :, :, 1].reshape(ny * NC * half, tall))
                first, second = block[:, 0], block[:, 1]
                rows_m = pl.ds(m * ny, ny)
                mine[g, rows_m] = jnp.where(c == 0, first, second)
                give[g, rows_m] = jnp.where(c == 0, second, first).astype(BF16)
        send(give.at[g], take.at[g], pair_sem.at[g], sibling)

    def add_pair(g):
        kind, n = groups[g]
        arrived(take.at[g], pair_sem.at[g])
        part[g] = (mine[g] + take[g].astype(F32)).astype(BF16)
        if kind == "up":
            for d in near_z:
                send(part.at[g, at_z(d)], recv_a.at[n, d - 1], ra_sem.at[n], to_z(d))
        else:
            for d in near_y:
                for m in range(2):
                    send(part.at[g, m * ny + at_y(d)], recv_b.at[n, d - 1, m], rb_sem.at[n], to_y(d))

    lag = 2
    for g in range(len(groups) + lag):
        if g < len(groups):
            terms(g)
        if g >= lag:
            add_pair(g - lag)

    loads[1].wait()
    loads[2].wait()
    delta[isl] = (anchor[...] - snapshot[...]).astype(BF16)
    for d in range(1, ni):
        send(delta.at[isl], delta.at[isl], delta_sem.at[isl], to_isl(d))

    kept = {}

    def add_up(g, n):
        arrived(recv_a.at[n], ra_sem.at[n])
        total = part[g, z].astype(F32) + jnp.sum(recv_a[n].astype(F32), axis=0)
        d = back_y[n]
        if d:
            send_a[n] = total.astype(BF16)
            send(send_a.at[n], last_a.at[d - 1], la_sem.at[0], to_y(d))
        else:
            kept["up"] = total

    def add_low(g, n):
        arrived(recv_b.at[n], rb_sem.at[n])
        for m, d in enumerate(pairs[n]):
            total = part[g, m * ny + y].astype(F32)
            for e in range(ny - 1):
                total = total + recv_b[n, e, m].astype(F32)
            if d:
                send_b[d - 1] = total.astype(BF16)
                send(send_b.at[d - 1], last_b.at[d - 1], lb_sem.at[0], to_z(d))
            else:
                kept["low"] = total

    for g, (kind, n) in enumerate(groups):
        if kind == "low":
            add_low(g, n)
        elif back_y[n]:
            add_up(g, n)
    add_up(len(groups) - 2, ny - 1)

    loads[4].wait()
    for d in range(1, ni):
        there = lax.rem(isl + d, ni)
        arrived(delta.at[there], delta_sem.at[there])
    delta_sum = delta[0].astype(F32)
    for n in range(1, ni):
        delta_sum = delta_sum + delta[n].astype(F32)
    mean_delta = delta_sum / float(ni)
    momentum_next = 0.9 * momentum[...] + mean_delta
    anchor_next = anchor[...] - 0.7 * (mean_delta + 0.9 * momentum_next)
    momentum_new_ref[...] = momentum_next
    anchor_new_ref[...] = anchor_next

    arrived(last_a, la_sem.at[0])
    summed[up, :] = kept["up"] + jnp.sum(last_a[...].astype(F32), axis=0)
    arrived(last_b, lb_sem.at[0])
    summed[low, :] = kept["low"] + jnp.sum(last_b[...].astype(F32), axis=0)
    for copy in sent:
        copy.wait_send()


def finish(
    dim,
    values,
    summed,
    anchor_new,
    momentum_new,
    weight,
    gain,
    first_w,
    second_w,
    first_g,
    second_g,
    values_out,
    weight_out,
    gain_out,
    first_w_out,
    second_w_out,
    first_g_out,
    second_g_out,
    anchor_out,
    momentum_out,
    weight_new,
    gain_new,
    first_w_new,
    second_w_new,
    first_g_new,
    second_g_new,
    sem,
):
    scale = 1.0 / float(dim) ** 0.5
    started = []

    def store(src, dst):
        copy = pltpu.make_async_copy(src, dst, sem.at[len(started)])
        copy.start()
        started.append(copy)

    store(values, values_out)
    store(anchor_new, anchor_out)
    store(momentum_new, momentum_out)
    grad = summed[...]
    old = weight[0]
    grad_weight = as_column(gain[...]) * grad * scale
    inner, first_w_new[0], second_w_new[0] = adamw(old, grad_weight, first_w[0], second_w[0])
    weight_new[0] = 0.5 * inner + 0.5 * anchor_new[...]
    store(weight_new, weight_out)
    store(first_w_new, first_w_out)
    store(second_w_new, second_w_out)
    grad_gain = as_row(jnp.sum(old * grad, axis=1, keepdims=True)) * scale
    gain_new[...], first_g_new[...], second_g_new[...] = adamw(gain[...], grad_gain, first_g[...], second_g[...])
    store(gain_new, gain_out)
    store(first_g_new, first_g_out)
    store(second_g_new, second_g_out)
    for copy in started:
        copy.wait()


def per_device(
    nz,
    ny,
    ni,
    tokens,
    target,
    weight,
    gain,
    first_weight,
    second_weight,
    first_gain,
    second_gain,
    anchor,
    snapshot,
    momentum,
):
    tall, dim = tokens.shape
    _, rows, head = weight.shape
    half = rows // 2
    vmem = pl.BlockSpec(memory_space=pltpu.VMEM)
    hbm = pl.BlockSpec(memory_space=pl.ANY)
    shard, line = (1, rows, head), (1, rows)
    whole = (rows, head)
    dma = pltpu.SemaphoreType.DMA
    sends = 2 * (nz - 1 + ny - 1) + 2 * (nz - 1) * (ny - 1) + nz
    sends += 2 * ny + ny * (nz - 1) + nz * (ny - 1) + (ni - 1) + (nz - 1) + (ny - 1)
    blocks = (2 * ny, nz, half, head)
    scratch = [
        pltpu.VMEM((tall, dim), BF16),
        pltpu.VMEM((nz, ny, NC, 2, half, tall), BF16),
        pltpu.VMEM((tall, head), BF16),
        *[pltpu.VMEM((rows, head), F32) for _ in range(4)],
        pltpu.VMEM(line, F32),
        pltpu.VMEM((rows, head), BF16),
        pltpu.VMEM((nz, ny, NC, rows, head), BF16),
        pltpu.VMEM((tall, head), F32),
        pltpu.VMEM((tall, head), F32),
        pltpu.VMEM((tall, head), BF16),
        pltpu.VMEM((ni, rows, head), BF16),
        pltpu.VMEM(blocks, F32),
        pltpu.VMEM(blocks, BF16),
        pltpu.VMEM(blocks, BF16),
        pltpu.VMEM(blocks, BF16),
        pltpu.VMEM((ny, nz - 1, half, head), BF16),
        pltpu.VMEM((ny, ny - 1, 2, half, head), BF16),
        pltpu.VMEM((ny - 1, half, head), BF16),
        pltpu.VMEM((nz - 1, half, head), BF16),
        pltpu.VMEM((ny - 1, half, head), BF16),
        pltpu.VMEM((nz - 1, half, head), BF16),
        dma((6,)),
        dma((nz,)),
        dma((sends,)),
        dma((nz,)),
        dma((ny,)),
        dma((nz,)),
        dma((nz,)),
        dma((nz,)),
        dma((ni,)),
        dma((2 * ny,)),
        dma((ny,)),
        dma((ny,)),
        dma((1,)),
        dma((1,)),
    ]

    def in_hbm(x):
        return pltpu.with_memory_space_constraint(x, pltpu.HBM)

    values, summed, anchor_new, momentum_new = pl.pallas_call(
        functools.partial(exchange, nz, ny, ni),
        out_shape=[
            pltpu.VMEM((tall, head), BF16),
            pltpu.VMEM(whole, F32),
            pltpu.VMEM(whole, F32),
            pltpu.VMEM(whole, F32),
        ],
        in_specs=[hbm] * 7,
        out_specs=[vmem] * 4,
        scratch_shapes=scratch,
        compiler_params=pltpu.CompilerParams(
            collective_id=0, has_side_effects=True, vmem_limit_bytes=24 * 2**20
        ),
        name="exchange",
    )(in_hbm(tokens), in_hbm(target), in_hbm(weight), in_hbm(gain), in_hbm(anchor), in_hbm(snapshot), in_hbm(momentum))
    shapes = [(tall, head), shard, line, shard, shard, line, line, whole, whole]
    return pl.pallas_call(
        functools.partial(finish, dim),
        out_shape=[pltpu.HBM(shape, F32 if n else BF16) for n, shape in enumerate(shapes)],
        in_specs=[vmem] * 10,
        out_specs=[hbm] * 9,
        scratch_shapes=[pltpu.VMEM(shape, F32) for shape in shapes[1:7]] + [dma((9,))],
        compiler_params=pltpu.CompilerParams(vmem_limit_bytes=8 * 2**20),
        name="finish",
    )(
        values,
        summed,
        anchor_new,
        momentum_new,
        weight,
        gain,
        first_weight,
        second_weight,
        first_gain,
        second_gain,
    )


def solution(mesh, nz=NZ, ny=NY):
    rows = P(("island", "fsdp"), None)
    shard = P("island", "fsdp", None)
    line = P("island", "fsdp")
    whole = P("fsdp", None)
    return jax.shard_map(
        functools.partial(per_device, nz, ny, mesh.shape["island"]),
        mesh=mesh,
        in_specs=(rows, rows, shard, line, shard, shard, line, line, whole, shard, whole),
        out_specs=(rows, shard, line, shard, shard, line, line, whole, whole),
        check_vma=False,
    )
```

time: 61.6 us -> 47.1 us (0.76)
  local copies, waits for them, and re-layouts: 14.9 us -> 0.03 us
  Pallas kernels: 45.4 us -> 46.2 us
    unnamed x31 -> x12, local copies, waits for them, and re-layouts: 14.9 us -> 0.03 us
    pallas_call x1 -> x2, Pallas kernels: 45.4 us -> 46.2 us  [the longest x1 45.3 us: per_device(): pl.pallas_call(functools.partial(exchange, nz, ny, ni), out_shape=[pltpu....]
where the time goes in v2:
time: 47.1 us; the launch traced here: 47 us
  Pallas kernels  46.2 us (98%)
  between operations  0.75 us (2%)
    pallas_call x1, Pallas kernels, per_device(): pl.pallas_call(functools.partial(exchange, nz, ny, ni), out_shape=[pltpu....  45.3 us

profile of v2, /device:TPU:1, one launch (start us, length us, event | category | flops | bytes accessed | tf_op | source)
XLA Modules:
  0.0 47.0 jit_solution(16185985798535626672)
XLA Ops:
  0.6 0.0 copy-start.3
  0.7 0.0 copy-start
  0.7 0.0 copy-start.5
  0.7 0.0 copy-start.4
  0.7 0.0 copy-start.2
  0.7 0.0 copy-start.1
  0.7 45.3 %exchange.1 = (bf16[512,128]{1,0:T(8,128)(2,1)S(1)}, f32[64,128]{1,0:T(8,128)S(1)}, f32[64,128]{1,0:T(8,128)S(1)}, f32[64,128]{1,0:T(8,128)S(1)}) custom-call(bf16[512,4096]{1,0:T(8,128)(2,1)} %tokens_hbm.1, bf16[512,128]{1,0:T(8,128)(2,1)} %target_hbm.1, f32[1,64,128]{2,1,0:T(8,128)} %weight.1, f32[1,64]{1,0:T(1,128)} %gain.1, f32[64,128]{1,0:T(8,128)} %anchor_hbm.1, ...), custom_call_target="tpu_custom_call" | custom-call | tf_op jit(solution)/shard_map/exchange/pallas_call | solution.py:482
  46.0 0.0 copy-done.3
  46.1 0.0 copy-done
  46.1 0.0 copy-done.5
  46.1 0.0 copy-done.4
  46.1 0.0 copy-done.2
  46.1 0.0 copy-done.1
  46.1 0.9 %finish.1 = (bf16[512,128]{1,0:T(8,128)(2,1)}, f32[1,64,128]{2,1,0:T(8,128)}, f32[1,64]{1,0:T(1,128)}, f32[1,64,128]{2,1,0:T(8,128)}, f32[1,64,128]{2,1,0:T(8,12...) custom-call(bf16[512,128]{1,0:T(8,128)(2,1)S(1)} %get-tuple-element.13.values, ...), custom_call_target="tpu_custom_call" | custom-call | tf_op jit(solution)/shard_map/finish/pallas_call | solution.py:499
Async XLA Ops:
  0.6 45.4 %copy-start.3 = (f32[1,64]{1,0:T(1,128)S(1)}, f32[1,64]{1,0:T(1,128)}, u32[]{:S(2)}) copy-start(f32[1,64]{1,0:T(1,128)} %gain.1) | copy-start | bytes 772
  0.7 45.4 %copy-start = (f32[1,64,128]{2,1,0:T(8,128)S(1)}, f32[1,64,128]{2,1,0:T(8,128)}, u32[]{:S(2)}) copy-start(f32[1,64,128]{2,1,0:T(8,128)} %weight.1) | copy-start | bytes 98308
  0.7 45.4 %copy-start.5 = (f32[1,64]{1,0:T(1,128)S(1)}, f32[1,64]{1,0:T(1,128)}, u32[]{:S(2)}) copy-start(f32[1,64]{1,0:T(1,128)} %second_g.1) | copy-start | bytes 772
  0.7 45.4 %copy-start.4 = (f32[1,64]{1,0:T(1,128)S(1)}, f32[1,64]{1,0:T(1,128)}, u32[]{:S(2)}) copy-start(f32[1,64]{1,0:T(1,128)} %first_g.1) | copy-start | bytes 772
  0.7 45.4 %copy-start.2 = (f32[1,64,128]{2,1,0:T(8,128)S(1)}, f32[1,64,128]{2,1,0:T(8,128)}, u32[]{:S(2)}) copy-start(f32[1,64,128]{2,1,0:T(8,128)} %second_w.1) | copy-start | bytes 98308
  0.7 45.4 %copy-start.1 = (f32[1,64,128]{2,1,0:T(8,128)S(1)}, f32[1,64,128]{2,1,0:T(8,128)}, u32[]{:S(2)}) copy-start(f32[1,64,128]{2,1,0:T(8,128)} %first_w.1) | copy-start | bytes 98308

commit v3 on v2

v3 whole, which is shorter than its diff:
```python
import functools

import jax
import jax.numpy as jnp
from jax import lax
from jax.experimental import pallas as pl
from jax.experimental.pallas import tpu as pltpu
from jax.sharding import PartitionSpec as P

MESH = pl.DeviceIdType.MESH
NZ, NY, NC = 8, 4, 2
F32, BF16 = jnp.float32, jnp.bfloat16


def ring_order(n):
    return sorted(range(1, n), key=lambda d: (min(d, n - d), d))


def spans(links, n):
    late = [links.count(1), sum(k < n // 2 for k in links), len(links)]
    cuts = [1] + sorted({1 + k for k in late})
    return list(zip(cuts[:-1], cuts[1:]))


def adamw(param, grad, first, second):
    first_next = 0.9 * first + 0.1 * grad
    second_next = 0.95 * second + 0.05 * grad * grad
    inner = param - 0.01 * (first_next / (jnp.sqrt(second_next) + 1e-08) + 0.1 * param)
    return inner, first_next, second_next


def eye(n):
    return lax.broadcasted_iota(jnp.int32, (n, n), 0) == lax.broadcasted_iota(jnp.int32, (n, n), 1)


def as_column(row):
    n = row.shape[1]
    return jnp.sum(jnp.where(eye(n), jnp.broadcast_to(row, (n, n)), 0.0), axis=1, keepdims=True)


def as_row(column):
    n = column.shape[0]
    return jnp.sum(jnp.where(eye(n), jnp.broadcast_to(column, (n, n)), 0.0), axis=0, keepdims=True)


def exchange(
    nz,
    ny,
    ni,
    tokens_hbm,
    target_hbm,
    weight_hbm,
    gain_hbm,
    anchor_hbm,
    snapshot_hbm,
    momentum_hbm,
    values_ref,
    summed,
    anchor_new_ref,
    momentum_new_ref,
    tok,
    halves,
    peer,
    target,
    target_t,
    weight,
    anchor,
    snapshot,
    momentum,
    gain_row,
    own,
    eff_a,
    eff_b,
    squares,
    acc,
    other,
    err_t,
    delta,
    part_a,
    part_b,
    recv_a,
    recv_b,
    send_a,
    send_b,
    last_a,
    last_b,
    load_sem,
    tok_sem,
    push_sem,
    peer_sem,
    send_sem,
    pair_sem,
    ya_sem,
    za_sem,
    zb_sem,
    yb_sem,
    delta_sem,
    ra_sem,
    rb_sem,
    la_sem,
    lb_sem,
):
    f = lax.axis_index("fsdp")
    isl = lax.axis_index("island")
    z, y, c = f // (ny * NC), (f // NC) % ny, f % NC
    rows, head = own.shape
    half = rows // 2
    tall = tok.shape[0]
    width = ny * NC * rows
    dim = tok.shape[1]
    up, low = pl.ds(0, half), pl.ds(half, half)
    near_z, near_y = ring_order(nz), ring_order(ny)
    back_z, back_y = near_z[::-1] + [0], near_y[::-1] + [0]
    place_z = {d: n for n, d in enumerate([0] + near_z)}
    hi, lo = y // 2, y % 2
    spans_z = spans([min(d, nz - d) for d in near_z], nz)
    spans_back_z = [(nz - stop, nz - max(start, 1)) for start, stop in spans_z[::-1]]
    spans_back_z[-1] = (spans_back_z[-1][0], nz)
    spans_back_y = [span for span in ((0, 1), (1, ny - 1), (ny - 1, ny)) if span[0] < span[1]]

    def at_z(d):
        return lax.rem(z + d, nz)

    def at_y(d):
        return lax.rem(y + d, ny)

    def to_z(d):
        return {"island": isl, "fsdp": (at_z(d) * ny + y) * NC + c}

    def to_y(d):
        return {"island": isl, "fsdp": (z * ny + at_y(d)) * NC + c}

    sibling = {"island": isl, "fsdp": (z * ny + y) * NC + 1 - c}

    def to_isl(d):
        return {"island": lax.rem(isl + d, ni), "fsdp": f}

    barrier = pltpu.get_barrier_semaphore()
    partners = [to_z(d) for d in near_z] + [to_y(d) for d in near_y] + [to_isl(d) for d in range(1, ni)] + [sibling]
    for partner in partners:
        pl.semaphore_signal(barrier, inc=1, device_id=partner, device_id_type=MESH)

    loads = [
        pltpu.make_async_copy(src, dst, load_sem.at[n])
        for n, (src, dst) in enumerate(
            [
                (weight_hbm.at[0], weight),
                (anchor_hbm, anchor),
                (snapshot_hbm.at[0], snapshot),
                (target_hbm, target.at[0]),
                (momentum_hbm, momentum),
                (gain_hbm, gain_row),
            ]
        )
    ]
    loads[5].start()
    loads[0].start()
    for k in range(nz):
        cols = pl.ds(k * width, width)
        pltpu.make_async_copy(tokens_hbm.at[:, cols], tok.at[:, cols], tok_sem.at[k]).start()
    for load in loads[1:5]:
        load.start()

    scale = 1.0 / float(dim) ** 0.5
    loads[5].wait()
    gain = as_column(gain_row[...])
    loads[0].wait()
    own[...] = (gain * weight[...] * scale).astype(BF16)
    eff_a[0, hi, lo] = own[up]
    eff_b[y, 0] = own[low]

    sent = []

    def send(src, dst, sem, device):
        copy = pltpu.make_async_remote_copy(
            src_ref=src,
            dst_ref=dst,
            send_sem=send_sem.at[len(sent)],
            recv_sem=sem,
            device_id=device,
            device_id_type=MESH,
        )
        copy.start()
        sent.append(copy)

    def arrived(ref, sem):
        pltpu.make_async_copy(ref, ref, sem).wait()

    pl.semaphore_wait(barrier, len(partners))

    for d in near_z:
        n = place_z[nz - d]
        send(own.at[low], eff_b.at[y, n], zb_sem.at[n], to_z(d))
    for d in near_y:
        send(own.at[up], eff_a.at[0, hi, lo], ya_sem.at[1 - d % 2], to_y(d))
    for d in near_z:
        send(own.at[up], eff_a.at[nz - d, hi, lo], za_sem.at[nz - d], to_z(d))
    for d in near_y:
        send(own.at[low], eff_b.at[y, 0], yb_sem.at[0], to_y(d))
    loads[3].wait()
    send(target.at[0], target.at[1], pair_sem.at[0], sibling)
    squares[0] = jnp.zeros((8, tall), F32)

    def push(k):
        return pltpu.make_async_remote_copy(
            src_ref=halves.at[k, 1 - c],
            dst_ref=peer.at[k],
            send_sem=push_sem.at[k],
            recv_sem=peer_sem.at[k],
            device_id=sibling,
            device_id_type=MESH,
        )

    def prepare(k, carry):
        cols = pl.ds(pl.multiple_of(k * width, width), width)
        pltpu.make_async_copy(tokens_hbm.at[:, cols], tok.at[:, cols], tok_sem.at[k]).wait()
        turned = tok[:, cols].T
        block = turned.reshape(ny, NC, rows, tall)
        for core in range(NC):
            halves[k, core] = block[:, core]
        push(k).start()
        wide = turned.astype(F32)
        squares[0] += jnp.sum((wide * wide).reshape(width // 8, 8, tall), axis=0)
        return carry

    def pass_low(g):
        start, stop = spans_z[g]
        for n in range(start, stop):
            arrived(eff_b.at[y, n], zb_sem.at[n])
        span = eff_b.at[y, pl.ds(start, stop - start)]
        for d in near_y:
            send(span, span, yb_sem.at[1 + g], to_y(d))

    def pass_up(other_parity):
        if other_parity:
            arrived(eff_a.at[0, :, 1 - lo], ya_sem.at[0])
        else:
            arrived(eff_a.at[0, 1 - hi, lo], ya_sem.at[1])
        for d in near_z:
            if other_parity:
                send(eff_a.at[0, :, 1 - lo], eff_a.at[nz - d, :, 1 - lo], za_sem.at[nz - d], to_z(d))
            else:
                send(eff_a.at[0, 1 - hi, lo], eff_a.at[nz - d, 1 - hi, lo], za_sem.at[nz - d], to_z(d))

    lax.fori_loop(0, nz // 2, prepare, 0)
    pass_low(0)
    lax.fori_loop(nz // 2, nz * 3 // 4, prepare, 0)
    pass_up(True)
    for g in range(1, len(spans_z) - 1):
        pass_low(g)
    if ny > 2:
        pass_up(False)
    pass_low(len(spans_z) - 1)
    lax.fori_loop(nz * 3 // 4, nz, prepare, 0)

    send(squares.at[0], squares.at[1], pair_sem.at[1], sibling)
    arrived(target.at[1], pair_sem.at[0])
    for n in range(2):
        target_t[n] = target[n].T
    arrived(squares.at[1], pair_sem.at[1])
    rstd = [lax.rsqrt(jnp.sum(squares[n], axis=0, keepdims=True) / float(dim) + 1e-05) for n in range(2)]

    for n, d in enumerate([0] + near_z):
        zb = at_z(d)
        if d:
            arrived(eff_a.at[d], za_sem.at[d])
        for g, (start, stop) in enumerate([(0, 1)] + spans_z):
            if n == start:
                arrived(eff_b.at[pl.ds(0, ny - 1), pl.ds(start, stop - start)], yb_sem.at[g])
        arrived(peer.at[zb], peer_sem.at[zb])
        upper = eff_a[d].reshape(ny, 1, half, head)
        block = jnp.concatenate([upper, eff_b[:, n][:, None]], axis=1).reshape(ny * rows, head)
        for m, side in enumerate((halves[zb, c], peer[zb])):
            partial = lax.dot_general(
                block, side.reshape(ny * rows, tall), (((0,), (0,)), ((), ())), preferred_element_type=F32
            )
            if n:
                acc[m] += partial
            else:
                acc[m] = partial
    for m in range(2):
        send(acc.at[m], other.at[1 - m], pair_sem.at[2 + m], sibling)

    def projected(m):
        return (acc[m] + other[m]) * rstd[m]

    for m in range(2):
        arrived(other.at[1 - m], pair_sem.at[2 + m])
    for m in range(2):
        err_t[m] = ((projected(m) - target_t[m].astype(F32)) * rstd[m]).astype(BF16)

    def product(left, right):
        total = None
        for m, side in enumerate((left, right)):
            term = lax.dot_general(
                side.reshape(-1, tall), err_t[m], (((1,), (1,)), ((), ())), preferred_element_type=F32
            )
            total = term if m == 0 else total + term
        return total.astype(BF16).reshape(-1, half, head)

    def terms_up(g):
        start, stop = spans_back_y[g]
        for n in range(start, stop):
            yb = at_y(back_y[n])
            part_a[:, n] = product(halves[:, c, yb, up], peer[:, yb, up])
        span = pl.ds(start, stop - start)
        for d in near_z:
            send(part_a.at[at_z(d), span], recv_a.at[d - 1, span], ra_sem.at[g], to_z(d))

    def terms_low(g):
        start, stop = spans_back_z[g]
        for n in range(start, stop):
            zb = at_z(back_z[n])
            part_b[:, n] = product(halves[zb, c, :, low], peer[zb, :, low])
        span = pl.ds(start, stop - start)
        for d in near_y:
            send(part_b.at[at_y(d), span], recv_b.at[d - 1, span], rb_sem.at[g], to_y(d))

    for g in range(3):
        if g < len(spans_back_z):
            terms_low(g)
        if g < len(spans_back_y):
            terms_up(g)

    loads[1].wait()
    loads[2].wait()
    delta[isl] = (anchor[...] - snapshot[...]).astype(BF16)
    for d in range(1, ni):
        send(delta.at[isl], delta.at[isl], delta_sem.at[isl], to_isl(d))

    values_ref[...] = projected(0).astype(BF16).T

    kept = {}

    def add_up(g):
        start, stop = spans_back_y[g]
        span = pl.ds(start, stop - start)
        arrived(recv_a.at[:, span], ra_sem.at[g])
        for n in range(start, stop):
            d = back_y[n]
            total = part_a[z, n].astype(F32) + jnp.sum(recv_a[:, n].astype(F32), axis=0)
            if d:
                send_a[n] = total.astype(BF16)
                send(send_a.at[n], last_a.at[d - 1], la_sem.at[0], to_y(d))
            else:
                kept["up"] = total

    def add_low(g):
        start, stop = spans_back_z[g]
        span = pl.ds(start, stop - start)
        arrived(recv_b.at[:, span], rb_sem.at[g])
        for n in range(start, stop):
            d = back_z[n]
            total = part_b[y, n].astype(F32) + jnp.sum(recv_b[:, n].astype(F32), axis=0)
            if d:
                send_b[d - 1] = total.astype(BF16)
                send(send_b.at[d - 1], last_b.at[d - 1], lb_sem.at[0], to_z(d))
            else:
                kept["low"] = total

    for g in range(3):
        if g < len(spans_back_z):
            add_low(g)
        if g < len(spans_back_y) - 1:
            add_up(g)
    add_up(len(spans_back_y) - 1)

    loads[4].wait()
    for d in range(1, ni):
        there = lax.rem(isl + d, ni)
        arrived(delta.at[there], delta_sem.at[there])
    delta_sum = delta[0].astype(F32)
    for n in range(1, ni):
        delta_sum = delta_sum + delta[n].astype(F32)
    mean_delta = delta_sum / float(ni)
    momentum_next = 0.9 * momentum[...] + mean_delta
    anchor_next = anchor[...] - 0.7 * (mean_delta + 0.9 * momentum_next)
    momentum_new_ref[...] = momentum_next
    anchor_new_ref[...] = anchor_next

    arrived(last_a, la_sem.at[0])
    summed[up, :] = kept["up"] + jnp.sum(last_a[...].astype(F32), axis=0)
    arrived(last_b, lb_sem.at[0])
    summed[low, :] = kept["low"] + jnp.sum(last_b[...].astype(F32), axis=0)
    for copy in sent:
        copy.wait_send()
    for k in range(nz):
        push(k).wait_send()


def finish(
    dim,
    values,
    summed,
    anchor_new,
    momentum_new,
    weight,
    gain,
    first_w,
    second_w,
    first_g,
    second_g,
    values_out,
    weight_out,
    gain_out,
    first_w_out,
    second_w_out,
    first_g_out,
    second_g_out,
    anchor_out,
    momentum_out,
    weight_new,
    gain_new,
    first_w_new,
    second_w_new,
    first_g_new,
    second_g_new,
    sem,
):
    scale = 1.0 / float(dim) ** 0.5
    started = []

    def store(src, dst):
        copy = pltpu.make_async_copy(src, dst, sem.at[len(started)])
        copy.start()
        started.append(copy)

    store(values, values_out)
    store(anchor_new, anchor_out)
    store(momentum_new, momentum_out)
    grad = summed[...]
    old = weight[0]
    grad_weight = as_column(gain[...]) * grad * scale
    inner, first_w_new[0], second_w_new[0] = adamw(old, grad_weight, first_w[0], second_w[0])
    weight_new[0] = 0.5 * inner + 0.5 * anchor_new[...]
    store(weight_new, weight_out)
    store(first_w_new, first_w_out)
    store(second_w_new, second_w_out)
    grad_gain = as_row(jnp.sum(old * grad, axis=1, keepdims=True)) * scale
    gain_new[...], first_g_new[...], second_g_new[...] = adamw(gain[...], grad_gain, first_g[...], second_g[...])
    store(gain_new, gain_out)
    store(first_g_new, first_g_out)
    store(second_g_new, second_g_out)
    for copy in started:
        copy.wait()


def per_device(
    nz,
    ny,
    ni,
    tokens,
    target,
    weight,
    gain,
    first_weight,
    second_weight,
    first_gain,
    second_gain,
    anchor,
    snapshot,
    momentum,
):
    tall, dim = tokens.shape
    _, rows, head = weight.shape
    half = rows // 2
    vmem = pl.BlockSpec(memory_space=pltpu.VMEM)
    hbm = pl.BlockSpec(memory_space=pl.ANY)
    shard, line = (1, rows, head), (1, rows)
    whole = (rows, head)
    dma = pltpu.SemaphoreType.DMA
    sends = 4 * (nz - 1) + 5 * (ny - 1) + 4
    sends += 4 * (nz - 1) + 4 * (ny - 1) + (ni - 1)
    scratch = [
        pltpu.VMEM((tall, dim), BF16),
        pltpu.VMEM((nz, NC, ny, rows, tall), BF16),
        pltpu.VMEM((nz, ny, rows, tall), BF16),
        pltpu.VMEM((2, tall, head), BF16),
        pltpu.VMEM((2, head, tall), BF16),
        *[pltpu.VMEM((rows, head), F32) for _ in range(4)],
        pltpu.VMEM(line, F32),
        pltpu.VMEM((rows, head), BF16),
        pltpu.VMEM((nz, ny // 2, 2, half, head), BF16),
        pltpu.VMEM((ny, nz, half, head), BF16),
        pltpu.VMEM((2, 8, tall), F32),
        pltpu.VMEM((2, head, tall), F32),
        pltpu.VMEM((2, head, tall), F32),
        pltpu.VMEM((2, head, tall), BF16),
        pltpu.VMEM((ni, rows, head), BF16),
        pltpu.VMEM((nz, ny, half, head), BF16),
        pltpu.VMEM((ny, nz, half, head), BF16),
        pltpu.VMEM((nz - 1, ny, half, head), BF16),
        pltpu.VMEM((ny - 1, nz, half, head), BF16),
        pltpu.VMEM((ny - 1, half, head), BF16),
        pltpu.VMEM((nz - 1, half, head), BF16),
        pltpu.VMEM((ny - 1, half, head), BF16),
        pltpu.VMEM((nz - 1, half, head), BF16),
        dma((6,)),
        dma((nz,)),
        dma((nz,)),
        dma((nz,)),
        dma((sends,)),
        dma((4,)),
        dma((2,)),
        dma((nz,)),
        dma((nz,)),
        dma((4,)),
        dma((ni,)),
        dma((3,)),
        dma((3,)),
        dma((1,)),
        dma((1,)),
    ]

    def in_hbm(x):
        return pltpu.with_memory_space_constraint(x, pltpu.HBM)

    values, summed, anchor_new, momentum_new = pl.pallas_call(
        functools.partial(exchange, nz, ny, ni),
        out_shape=[
            pltpu.VMEM((tall, head), BF16),
            pltpu.VMEM(whole, F32),
            pltpu.VMEM(whole, F32),
            pltpu.VMEM(whole, F32),
        ],
        in_specs=[hbm] * 7,
        out_specs=[vmem] * 4,
        scratch_shapes=scratch,
        compiler_params=pltpu.CompilerParams(
            collective_id=0, has_side_effects=True, vmem_limit_bytes=24 * 2**20
        ),
        name="exchange",
    )(in_hbm(tokens), in_hbm(target), in_hbm(weight), in_hbm(gain), in_hbm(anchor), in_hbm(snapshot), in_hbm(momentum))
    shapes = [(tall, head), shard, line, shard, shard, line, line, whole, whole]
    return pl.pallas_call(
        functools.partial(finish, dim),
        out_shape=[pltpu.HBM(shape, F32 if n else BF16) for n, shape in enumerate(shapes)],
        in_specs=[vmem] * 10,
        out_specs=[hbm] * 9,
        scratch_shapes=[pltpu.VMEM(shape, F32) for shape in shapes[1:7]] + [dma((9,))],
        compiler_params=pltpu.CompilerParams(vmem_limit_bytes=8 * 2**20),
        name="finish",
    )(
        values,
        summed,
        anchor_new,
        momentum_new,
        weight,
        gain,
        first_weight,
        second_weight,
        first_gain,
        second_gain,
    )


def solution(mesh, nz=NZ, ny=NY):
    rows = P(("island", "fsdp"), None)
    shard = P("island", "fsdp", None)
    line = P("island", "fsdp")
    whole = P("fsdp", None)
    return jax.shard_map(
        functools.partial(per_device, nz, ny, mesh.shape["island"]),
        mesh=mesh,
        in_specs=(rows, rows, shard, line, shard, shard, line, line, whole, shard, whole),
        out_specs=(rows, shard, line, shard, shard, line, line, whole, whole),
        check_vma=False,
    )
```

time: 47.1 us -> 43.2 us (0.917)
  Pallas kernels: 46.2 us -> 42.3 us
    pallas_call x1, Pallas kernels: 45.3 us -> 41.4 us  [per_device(): pl.pallas_call(functools.partial(exchange, nz, ny, ni), out_shape=[pltpu....]
where the time goes in v3:
time: 43.2 us; the launch traced here: 43.1 us
  Pallas kernels  42.3 us (98%)
  between operations  0.75 us (2%)
    pallas_call x1, Pallas kernels, per_device(): pl.pallas_call(functools.partial(exchange, nz, ny, ni), out_shape=[pltpu....  41.4 us

profile of v3, /device:TPU:1, one launch (start us, length us, event | category | flops | bytes accessed | tf_op | source)
XLA Modules:
  0.0 43.1 jit_solution(544906929671183975)
XLA Ops:
  0.6 0.0 copy-start.3
  0.7 0.0 copy-start
  0.7 0.0 copy-start.5
  0.7 0.0 copy-start.4
  0.7 0.0 copy-start.2
  0.7 0.0 copy-start.1
  0.7 41.4 %exchange.1 = (bf16[512,128]{1,0:T(8,128)(2,1)S(1)}, f32[64,128]{1,0:T(8,128)S(1)}, f32[64,128]{1,0:T(8,128)S(1)}, f32[64,128]{1,0:T(8,128)S(1)}) custom-call(bf16[512,4096]{1,0:T(8,128)(2,1)} %tokens_hbm.1, bf16[512,128]{1,0:T(8,128)(2,1)} %target_hbm.1, f32[1,64,128]{2,1,0:T(8,128)} %weight.1, f32[1,64]{1,0:T(1,128)} %gain.1, f32[64,128]{1,0:T(8,128)} %anchor_hbm.1, ...), custom_call_target="tpu_custom_call" | custom-call | tf_op jit(solution)/shard_map/exchange/pallas_call | solution.py:518
  42.2 0.0 copy-done.3
  42.2 0.0 copy-done
  42.2 0.0 copy-done.5
  42.2 0.0 copy-done.4
  42.2 0.0 copy-done.2
  42.2 0.0 copy-done.1
  42.2 0.9 %finish.1 = (bf16[512,128]{1,0:T(8,128)(2,1)}, f32[1,64,128]{2,1,0:T(8,128)}, f32[1,64]{1,0:T(1,128)}, f32[1,64,128]{2,1,0:T(8,128)}, f32[1,64,128]{2,1,0:T(8,12...) custom-call(bf16[512,128]{1,0:T(8,128)(2,1)S(1)} %get-tuple-element.13.values, ...), custom_call_target="tpu_custom_call" | custom-call | tf_op jit(solution)/shard_map/finish/pallas_call | solution.py:535
Async XLA Ops:
  0.6 41.5 %copy-start.3 = (f32[1,64]{1,0:T(1,128)S(1)}, f32[1,64]{1,0:T(1,128)}, u32[]{:S(2)}) copy-start(f32[1,64]{1,0:T(1,128)} %gain.1) | copy-start | bytes 772
  0.7 41.5 %copy-start = (f32[1,64,128]{2,1,0:T(8,128)S(1)}, f32[1,64,128]{2,1,0:T(8,128)}, u32[]{:S(2)}) copy-start(f32[1,64,128]{2,1,0:T(8,128)} %weight.1) | copy-start | bytes 98308
  0.7 41.5 %copy-start.5 = (f32[1,64]{1,0:T(1,128)S(1)}, f32[1,64]{1,0:T(1,128)}, u32[]{:S(2)}) copy-start(f32[1,64]{1,0:T(1,128)} %second_g.1) | copy-start | bytes 772
  0.7 41.5 %copy-start.4 = (f32[1,64]{1,0:T(1,128)S(1)}, f32[1,64]{1,0:T(1,128)}, u32[]{:S(2)}) copy-start(f32[1,64]{1,0:T(1,128)} %first_g.1) | copy-start | bytes 772
  0.7 41.5 %copy-start.2 = (f32[1,64,128]{2,1,0:T(8,128)S(1)}, f32[1,64,128]{2,1,0:T(8,128)}, u32[]{:S(2)}) copy-start(f32[1,64,128]{2,1,0:T(8,128)} %second_w.1) | copy-start | bytes 98308
  0.7 41.5 %copy-start.1 = (f32[1,64,128]{2,1,0:T(8,128)S(1)}, f32[1,64,128]{2,1,0:T(8,128)}, u32[]{:S(2)}) copy-start(f32[1,64,128]{2,1,0:T(8,128)} %first_w.1) | copy-start | bytes 98308

commit v4 on v3

--- a/solution.py
+++ b/solution.py
@@ -136,7 +136,7 @@
         return {"island": lax.rem(isl + d, ni), "fsdp": f}
 
     barrier = pltpu.get_barrier_semaphore()
-    partners = [to_z(d) for d in near_z] + [to_y(d) for d in near_y] + [to_isl(d) for d in range(1, ni)] + [sibling]
+    partners = [to_z(d) for d in near_z[::-1]] + [to_y(d) for d in near_y] + [to_isl(d) for d in range(1, ni)] + [sibling]
     for partner in partners:
         pl.semaphore_signal(barrier, inc=1, device_id=partner, device_id_type=MESH)
 
@@ -242,16 +242,16 @@
             else:
                 send(eff_a.at[0, 1 - hi, lo], eff_a.at[nz - d, 1 - hi, lo], za_sem.at[nz - d], to_z(d))
 
-    lax.fori_loop(0, nz // 2, prepare, 0)
+    lax.fori_loop(0, nz // 4, prepare, 0)
     pass_low(0)
-    lax.fori_loop(nz // 2, nz * 3 // 4, prepare, 0)
+    lax.fori_loop(nz // 4, nz // 2, prepare, 0)
     pass_up(True)
     for g in range(1, len(spans_z) - 1):
         pass_low(g)
     if ny > 2:
         pass_up(False)
     pass_low(len(spans_z) - 1)
-    lax.fori_loop(nz * 3 // 4, nz, prepare, 0)
+    lax.fori_loop(nz // 2, nz, prepare, 0)
 
     send(squares.at[0], squares.at[1], pair_sem.at[1], sibling)
     arrived(target.at[1], pair_sem.at[0])
@@ -304,7 +304,7 @@
             yb = at_y(back_y[n])
             part_a[:, n] = product(halves[:, c, yb, up], peer[:, yb, up])
         span = pl.ds(start, stop - start)
-        for d in near_z:
+        for d in near_z[::-1]:
             send(part_a.at[at_z(d), span], recv_a.at[d - 1, span], ra_sem.at[g], to_z(d))
 
     def terms_low(g):
@@ -313,14 +313,15 @@
             zb = at_z(back_z[n])
             part_b[:, n] = product(halves[zb, c, :, low], peer[zb, :, low])
         span = pl.ds(start, stop - start)
-        for d in near_y:
+        for d in near_y[::-1]:
             send(part_b.at[at_y(d), span], recv_b.at[d - 1, span], rb_sem.at[g], to_y(d))
 
-    for g in range(3):
-        if g < len(spans_back_z):
-            terms_low(g)
-        if g < len(spans_back_y):
-            terms_up(g)
+    terms_low(0)
+    terms_low(1)
+    terms_up(0)
+    terms_low(2)
+    terms_up(1)
+    terms_up(2)
 
     loads[1].wait()
     loads[2].wait()

time: 43.2 us -> 42.5 us (0.984)
  Pallas kernels: 42.3 us -> 41.5 us
    pallas_call x1, Pallas kernels: 41.4 us -> 40.7 us  [per_device(): pl.pallas_call(functools.partial(exchange, nz, ny, ni), out_shape=[pltpu....]
where the time goes in v4:
time: 42.5 us; the launch traced here: 42.3 us
  Pallas kernels  41.5 us (98%)
  between operations  0.75 us (2%)
    pallas_call x1, Pallas kernels, per_device(): pl.pallas_call(functools.partial(exchange, nz, ny, ni), out_shape=[pltpu....  40.7 us
    pallas_call x1, Pallas kernels, per_device(): pl.pallas_call(functools.partial(finish, dim), out_shape=[pltpu.HBM(shape...  0.85 us

profile of v4, /device:TPU:1, one launch (start us, length us, event | category | flops | bytes accessed | tf_op | source)
XLA Modules:
  0.0 42.3 jit_solution(18124007046928391671)
XLA Ops:
  0.6 0.0 copy-start.3
  0.7 0.0 copy-start
  0.7 0.0 copy-start.5
  0.7 0.0 copy-start.4
  0.7 0.0 copy-start.2
  0.7 0.0 copy-start.1
  0.7 40.7 %exchange.1 = (bf16[512,128]{1,0:T(8,128)(2,1)S(1)}, f32[64,128]{1,0:T(8,128)S(1)}, f32[64,128]{1,0:T(8,128)S(1)}, f32[64,128]{1,0:T(8,128)S(1)}) custom-call(bf16[512,4096]{1,0:T(8,128)(2,1)} %tokens_hbm.1, bf16[512,128]{1,0:T(8,128)(2,1)} %target_hbm.1, f32[1,64,128]{2,1,0:T(8,128)} %weight.1, f32[1,64]{1,0:T(1,128)} %gain.1, f32[64,128]{1,0:T(8,128)} %anchor_hbm.1, ...), custom_call_target="tpu_custom_call" | custom-call | tf_op jit(solution)/shard_map/exchange/pallas_call | solution.py:519
  41.4 0.0 copy-done.3
  41.4 0.0 copy-done
  41.4 0.0 copy-done.5
  41.4 0.0 copy-done.4
  41.4 0.0 copy-done.2
  41.4 0.0 copy-done.1
  41.5 0.9 %finish.1 = (bf16[512,128]{1,0:T(8,128)(2,1)}, f32[1,64,128]{2,1,0:T(8,128)}, f32[1,64]{1,0:T(1,128)}, f32[1,64,128]{2,1,0:T(8,128)}, f32[1,64,128]{2,1,0:T(8,12...) custom-call(bf16[512,128]{1,0:T(8,128)(2,1)S(1)} %get-tuple-element.13.values, ...), custom_call_target="tpu_custom_call" | custom-call | tf_op jit(solution)/shard_map/finish/pallas_call | solution.py:536
Async XLA Ops:
  0.6 40.7 %copy-start.3 = (f32[1,64]{1,0:T(1,128)S(1)}, f32[1,64]{1,0:T(1,128)}, u32[]{:S(2)}) copy-start(f32[1,64]{1,0:T(1,128)} %gain.1) | copy-start | bytes 772
  0.7 40.7 %copy-start = (f32[1,64,128]{2,1,0:T(8,128)S(1)}, f32[1,64,128]{2,1,0:T(8,128)}, u32[]{:S(2)}) copy-start(f32[1,64,128]{2,1,0:T(8,128)} %weight.1) | copy-start | bytes 98308
  0.7 40.7 %copy-start.5 = (f32[1,64]{1,0:T(1,128)S(1)}, f32[1,64]{1,0:T(1,128)}, u32[]{:S(2)}) copy-start(f32[1,64]{1,0:T(1,128)} %second_g.1) | copy-start | bytes 772
  0.7 40.7 %copy-start.4 = (f32[1,64]{1,0:T(1,128)S(1)}, f32[1,64]{1,0:T(1,128)}, u32[]{:S(2)}) copy-start(f32[1,64]{1,0:T(1,128)} %first_g.1) | copy-start | bytes 772
  0.7 40.7 %copy-start.2 = (f32[1,64,128]{2,1,0:T(8,128)S(1)}, f32[1,64,128]{2,1,0:T(8,128)}, u32[]{:S(2)}) copy-start(f32[1,64,128]{2,1,0:T(8,128)} %second_w.1) | copy-start | bytes 98308
  0.7 40.7 %copy-start.1 = (f32[1,64,128]{2,1,0:T(8,128)S(1)}, f32[1,64,128]{2,1,0:T(8,128)}, u32[]{:S(2)}) copy-start(f32[1,64,128]{2,1,0:T(8,128)} %first_w.1) | copy-start | bytes 98308

commit v5 on v4

--- a/solution.py
+++ b/solution.py
@@ -270,7 +270,8 @@
         arrived(peer.at[zb], peer_sem.at[zb])
         upper = eff_a[d].reshape(ny, 1, half, head)
         block = jnp.concatenate([upper, eff_b[:, n][:, None]], axis=1).reshape(ny * rows, head)
-        for m, side in enumerate((halves[zb, c], peer[zb])):
+        for m in (1, 0):
+            side = peer[zb] if m else halves[zb, c]
             partial = lax.dot_general(
                 block, side.reshape(ny * rows, tall), (((0,), (0,)), ((), ())), preferred_element_type=F32
             )
@@ -278,15 +279,14 @@
                 acc[m] += partial
             else:
                 acc[m] = partial
-    for m in range(2):
-        send(acc.at[m], other.at[1 - m], pair_sem.at[2 + m], sibling)
+            if n == nz - 1:
+                send(acc.at[m], other.at[1 - m], pair_sem.at[2 + m], sibling)
 
     def projected(m):
         return (acc[m] + other[m]) * rstd[m]
 
     for m in range(2):
-        arrived(other.at[1 - m], pair_sem.at[2 + m])
-    for m in range(2):
+        arrived(other.at[m], pair_sem.at[3 - m])
         err_t[m] = ((projected(m) - target_t[m].astype(F32)) * rstd[m]).astype(BF16)
 
     def product(left, right):

time: 42.5 us -> 43.1 us (1.014)
  Pallas kernels: 41.5 us -> 42.1 us
    pallas_call x1, Pallas kernels: 40.7 us -> 41.3 us  [per_device(): pl.pallas_call(functools.partial(exchange, nz, ny, ni), out_shape=[pltpu....]
where the time goes in v5:
time: 43.1 us; the launch traced here: 42.9 us
  Pallas kernels  42.1 us (98%)
  between operations  0.75 us (2%)
    pallas_call x1, Pallas kernels, per_device(): pl.pallas_call(functools.partial(exchange, nz, ny, ni), out_shape=[pltpu....  41.3 us

profile of v5, /device:TPU:1, one launch (start us, length us, event | category | flops | bytes accessed | tf_op | source)
XLA Modules:
  0.0 42.9 jit_solution(12594652775433997392)
XLA Ops:
  0.6 0.0 copy-start.3
  0.7 0.0 copy-start
  0.7 0.0 copy-start.5
  0.7 0.0 copy-start.4
  0.7 0.0 copy-start.2
  0.7 0.0 copy-start.1
  0.7 41.3 %exchange.1 = (bf16[512,128]{1,0:T(8,128)(2,1)S(1)}, f32[64,128]{1,0:T(8,128)S(1)}, f32[64,128]{1,0:T(8,128)S(1)}, f32[64,128]{1,0:T(8,128)S(1)}) custom-call(bf16[512,4096]{1,0:T(8,128)(2,1)} %tokens_hbm.1, bf16[512,128]{1,0:T(8,128)(2,1)} %target_hbm.1, f32[1,64,128]{2,1,0:T(8,128)} %weight.1, f32[1,64]{1,0:T(1,128)} %gain.1, f32[64,128]{1,0:T(8,128)} %anchor_hbm.1, ...), custom_call_target="tpu_custom_call" | custom-call | tf_op jit(solution)/shard_map/exchange/pallas_call | solution.py:519
  42.0 0.0 copy-done.3
  42.0 0.0 copy-done
  42.0 0.0 copy-done.5
  42.0 0.0 copy-done.4
  42.0 0.0 copy-done.2
  42.0 0.0 copy-done.1
  42.0 0.9 %finish.1 = (bf16[512,128]{1,0:T(8,128)(2,1)}, f32[1,64,128]{2,1,0:T(8,128)}, f32[1,64]{1,0:T(1,128)}, f32[1,64,128]{2,1,0:T(8,128)}, f32[1,64,128]{2,1,0:T(8,12...) custom-call(bf16[512,128]{1,0:T(8,128)(2,1)S(1)} %get-tuple-element.13.values, ...), custom_call_target="tpu_custom_call" | custom-call | tf_op jit(solution)/shard_map/finish/pallas_call | solution.py:536
Async XLA Ops:
  0.6 41.3 %copy-start.3 = (f32[1,64]{1,0:T(1,128)S(1)}, f32[1,64]{1,0:T(1,128)}, u32[]{:S(2)}) copy-start(f32[1,64]{1,0:T(1,128)} %gain.1) | copy-start | bytes 772
  0.7 41.3 %copy-start = (f32[1,64,128]{2,1,0:T(8,128)S(1)}, f32[1,64,128]{2,1,0:T(8,128)}, u32[]{:S(2)}) copy-start(f32[1,64,128]{2,1,0:T(8,128)} %weight.1) | copy-start | bytes 98308
  0.7 41.3 %copy-start.5 = (f32[1,64]{1,0:T(1,128)S(1)}, f32[1,64]{1,0:T(1,128)}, u32[]{:S(2)}) copy-start(f32[1,64]{1,0:T(1,128)} %second_g.1) | copy-start | bytes 772
  0.7 41.3 %copy-start.4 = (f32[1,64]{1,0:T(1,128)S(1)}, f32[1,64]{1,0:T(1,128)}, u32[]{:S(2)}) copy-start(f32[1,64]{1,0:T(1,128)} %first_g.1) | copy-start | bytes 772
  0.7 41.3 %copy-start.2 = (f32[1,64,128]{2,1,0:T(8,128)S(1)}, f32[1,64,128]{2,1,0:T(8,128)}, u32[]{:S(2)}) copy-start(f32[1,64,128]{2,1,0:T(8,128)} %second_w.1) | copy-start | bytes 98308
  0.7 41.3 %copy-start.1 = (f32[1,64,128]{2,1,0:T(8,128)S(1)}, f32[1,64,128]{2,1,0:T(8,128)}, u32[]{:S(2)}) copy-start(f32[1,64,128]{2,1,0:T(8,128)} %first_w.1) | copy-start | bytes 98308
